TPU v7x, 32 devices: a whole 2x2x4 slice. The times are simulated.
32 devices in a mesh: dp: 4 (over y, x), vocab: 8 (over z, core).
Axes of the slice: x: 2, y: 2, z: 4, core: 2. Of those that a mesh axis runs over, the one named last changes fastest.
Arguments:
- token_ids: int32 [32768], P(('dp', 'vocab')), may hold values from 0 to 32127, as said below
- seq_lengths: int32 [64], P(('dp', 'vocab')), may hold values from 1 to 512, 24576 in all
- table: bfloat16 [32128, 768], P('vocab'), may hold values from -6 to 6
- gain_one: float32 [768], replicated, may hold values from 0.5 to 1.5
- w_query: bfloat16 [768, 768], replicated, may hold values from -0.078125 to 0.078125
- w_key: bfloat16 [768, 768], replicated, may hold values from -0.078125 to 0.078125
- w_value: bfloat16 [768, 768], replicated, may hold values from -0.21875 to 0.21875
- w_out: bfloat16 [768, 768], replicated, may hold values from -2.5 to 2.5
- gain_two: float32 [768], replicated, may hold values from 0.5 to 1.5
- w_in: bfloat16 [768, 3072], replicated, may hold values from -0.21875 to 0.21875
- w_down: bfloat16 [3072, 768], replicated, may hold values from -0.109375 to 0.109375
- rel_bias: float32 [32, 12], replicated, may hold values from -6 to 6
- cotangent: bfloat16 [32768, 768], P(('dp', 'vocab')), may hold values from -6 to 6
Outputs:
- mixed_out: bfloat16 [32768, 768], P(('dp', 'vocab'))
- row_grad: float32 [32768, 768], P(('dp', 'vocab'))
- table_grad: float32 [32128, 768], P('vocab')
- gain_one_grad: float32 [768], replicated
- query_grad: float32 [768, 768], P('dp', 'vocab')
- key_grad: float32 [768, 768], P('dp', 'vocab')
- value_grad: float32 [768, 768], P('dp', 'vocab')
- out_grad: float32 [768, 768], P('dp', 'vocab')
- gain_two_grad: float32 [768], replicated
- in_grad: float32 [768, 3072], P('dp', 'vocab')
- down_grad: float32 [3072, 768], P('dp', 'vocab')
- bias_grad: float32 [32, 12], replicated
Inputs may be any that keep to these rules, and one draw needn't show every extreme that they name: `token_ids`: ids are table rows. Among the 1024 ids of one device at most 256 lie in the range of one index o of vocab (ids o * 4016 to o * 4016 + 4015), and exactly 256 lie in one such range: the 128 ids of the instruction that opens each of the device's sequences, the same in all of them.
All inputs are finite; a program needn't handle non-finite values. No bound on the sum of `seq_lengths` on one device may be relied on, other than what follows from the above.
Results may differ from a plain program's by a relative error of at most 0.015.
Values may be sent and summed in bfloat16 or wider, within the bound.
No kernel may reach another device: no remote copies, remote signals or barrier semaphores. Data moves between devices by JAX's collectives and lax.ppermute only.
A program may use at most 256 MiB of HBM per device.

v0:
```python
from functools import partial

import jax
import jax.numpy as jnp
from jax import lax
from jax.sharding import PartitionSpec as P

EPS = 1e-06
PRECISE = lax.Precision.HIGHEST
MASKED = -1e30
THRESHOLDS = (12, 16, 23, 32, 46, 64, 91)


def norm_apply(values, gain_vec):
    scaling = lax.rsqrt(jnp.mean(values * values, axis=-1, keepdims=True) + EPS)
    return values * scaling * gain_vec


def gelu_tanh(values):
    return jax.nn.gelu(values, approximate=True)


def bucket_onehot(length, bucket_count):
    places = jnp.arange(length, dtype=jnp.int32)
    offset = places[None, :] - places[:, None]
    distance = jnp.abs(offset)
    far_bucket = jnp.full_like(distance, 8)
    for threshold in THRESHOLDS:
        far_bucket = far_bucket + (distance >= threshold).astype(jnp.int32)
    upper = jnp.where(offset > 0, 16, 0).astype(jnp.int32)
    bucket = upper + jnp.where(distance < 8, distance, far_bucket)
    labels = jnp.arange(bucket_count, dtype=jnp.int32)
    return (labels[:, None] == bucket.reshape(1, -1)).astype(jnp.float32)


def masked_scores(query_in, keys_in, length, bias_full):
    raw_scores = jnp.einsum("qhe,khe->hqk", query_in, keys_in, preferred_element_type=jnp.float32)
    seq_len = query_in.shape[0]
    allowed = jnp.arange(seq_len, dtype=jnp.int32)[None, None, :] < length
    return jnp.where(allowed, raw_scores + bias_full, MASKED)


def attend_forward(pieces, bias_full):
    query_in, keys_in, values_in, length = pieces
    scores = masked_scores(query_in, keys_in, length, bias_full)
    highest = jnp.max(scores, axis=-1, keepdims=True)
    exponent = jnp.exp(scores - highest)
    totals = jnp.sum(exponent, axis=-1, keepdims=True)
    probs_low = (exponent / totals).astype(jnp.bfloat16)
    context = jnp.einsum("hqk,khe->qhe", probs_low, values_in, preferred_element_type=jnp.float32)
    return (context.astype(jnp.bfloat16), (highest + jnp.log(totals))[..., 0])


def attend_backward(pieces, bias_full, onehot):
    query_in, keys_in, values_in, length, log_total, d_context = pieces
    scores = masked_scores(query_in, keys_in, length, bias_full)
    probs_full = jnp.exp(scores - log_total[..., None])
    d_probs = jnp.einsum("qhe,khe->hqk", d_context, values_in, preferred_element_type=jnp.float32)
    d_scores = probs_full * (d_probs - jnp.sum(probs_full * d_probs, axis=-1, keepdims=True))
    d_low = d_scores.astype(jnp.bfloat16)
    d_query = jnp.einsum("hqk,khe->qhe", d_low, keys_in, preferred_element_type=jnp.float32)
    d_keys = jnp.einsum("hqk,qhe->khe", d_low, query_in, preferred_element_type=jnp.float32)
    d_values = jnp.einsum(
        "hqk,qhe->khe",
        probs_full.astype(jnp.bfloat16),
        d_context,
        preferred_element_type=jnp.float32,
    )
    head_count = d_scores.shape[0]
    bias_part = jnp.einsum("hn,bn->hb", d_scores.reshape(head_count, -1), onehot, precision=PRECISE)
    return (
        d_query.astype(jnp.bfloat16),
        d_keys.astype(jnp.bfloat16),
        d_values.astype(jnp.bfloat16),
        bias_part,
    )


def body(
    token_ids,
    seq_lengths,
    table,
    gain_one,
    w_query,
    w_key,
    w_value,
    w_out,
    gain_two,
    w_in,
    w_down,
    rel_bias,
    cotangent,
):
    owners = lax.axis_size("vocab")
    shard_rows = table.shape[0]
    model_width = table.shape[1]
    tok_count = token_ids.shape[0]
    seq_count = seq_lengths.shape[0]
    seq_len = tok_count // seq_count
    head_count = rel_bias.shape[1]
    head_dim = model_width // head_count
    capacity = max(2, 2 * tok_count // owners)
    block_shape = (seq_count, seq_len, head_count, head_dim)
    owner_of = token_ids // shard_rows
    member = (owner_of[:, None] == jnp.arange(owners, dtype=jnp.int32)[None, :]).astype(
        jnp.bfloat16
    )
    places = jnp.arange(tok_count, dtype=jnp.int32)
    earlier = (places[:, None] > places[None, :]).astype(jnp.bfloat16)
    counts = jnp.dot(earlier, member, preferred_element_type=jnp.float32)
    slot_rank = jnp.sum(counts * member.astype(jnp.float32), axis=1).astype(jnp.int32)
    slot_index = owner_of * capacity + slot_rank
    request = (
        jnp.full((owners * capacity,), -1, jnp.int32)
        .at[slot_index]
        .set(token_ids)
        .reshape(owners, capacity)
    )
    base_row = lax.axis_index("vocab") * shard_rows
    asked_ids = lax.all_to_all(request, "vocab", split_axis=0, concat_axis=0, tiled=True)
    present = asked_ids >= 0
    local_row = jnp.clip(asked_ids - base_row, 0, shard_rows - 1)
    picked = jnp.where(
        present[..., None], jnp.take(table, local_row, axis=0), jnp.zeros((), jnp.bfloat16)
    )
    returned = lax.all_to_all(picked, "vocab", split_axis=0, concat_axis=0, tiled=True)
    x_rows = returned.reshape(owners * capacity, model_width)[slot_index].astype(jnp.float32)
    normed_one, pull_one = jax.vjp(norm_apply, x_rows, gain_one)
    hidden = normed_one.astype(jnp.bfloat16)
    query_all = jnp.dot(hidden, w_query, preferred_element_type=jnp.float32).astype(jnp.bfloat16)
    keys_all = jnp.dot(hidden, w_key, preferred_element_type=jnp.float32).astype(jnp.bfloat16)
    values_all = jnp.dot(hidden, w_value, preferred_element_type=jnp.float32).astype(jnp.bfloat16)
    onehot = bucket_onehot(seq_len, rel_bias.shape[0])
    bias_full = jnp.dot(rel_bias.T, onehot, precision=PRECISE).reshape(head_count, seq_len, seq_len)
    query_seq = query_all.reshape(block_shape)
    keys_seq = keys_all.reshape(block_shape)
    values_seq = values_all.reshape(block_shape)
    context, log_total = lax.map(
        partial(attend_forward, bias_full=bias_full), (query_seq, keys_seq, values_seq, seq_lengths)
    )
    context_flat = context.reshape(tok_count, model_width)
    middle = x_rows + jnp.dot(context_flat, w_out, preferred_element_type=jnp.float32)
    normed_two, pull_two = jax.vjp(norm_apply, middle, gain_two)
    hidden_two = normed_two.astype(jnp.bfloat16)
    pre_act = jnp.dot(hidden_two, w_in, preferred_element_type=jnp.float32)
    act_full, pull_act = jax.vjp(gelu_tanh, pre_act)
    act_low = act_full.astype(jnp.bfloat16)
    mixed_out = (middle + jnp.dot(act_low, w_down, preferred_element_type=jnp.float32)).astype(
        jnp.bfloat16
    )
    down_grad = jnp.einsum("tf,td->fd", act_low, cotangent, preferred_element_type=jnp.float32)
    d_act = jnp.dot(cotangent, w_down.T, preferred_element_type=jnp.float32)
    d_pre = pull_act(d_act)[0]
    d_pre_low = d_pre.astype(jnp.bfloat16)
    in_grad = jnp.einsum("td,tf->df", hidden_two, d_pre_low, preferred_element_type=jnp.float32)
    d_hidden_two = jnp.dot(d_pre_low, w_in.T, preferred_element_type=jnp.float32)
    d_norm_two, gain_two_grad = pull_two(d_hidden_two)
    d_middle = cotangent.astype(jnp.float32) + d_norm_two
    d_attended = d_middle.astype(jnp.bfloat16)
    out_grad = jnp.einsum("td,te->de", context_flat, d_attended, preferred_element_type=jnp.float32)
    d_context = jnp.dot(d_attended, w_out.T, preferred_element_type=jnp.float32).astype(
        jnp.bfloat16
    )
    d_query, d_keys, d_values, bias_parts = lax.map(
        partial(attend_backward, bias_full=bias_full, onehot=onehot),
        (query_seq, keys_seq, values_seq, seq_lengths, log_total, d_context.reshape(block_shape)),
    )
    d_query = d_query.reshape(tok_count, model_width)
    d_keys = d_keys.reshape(tok_count, model_width)
    d_values = d_values.reshape(tok_count, model_width)
    query_grad = jnp.einsum("td,te->de", hidden, d_query, preferred_element_type=jnp.float32)
    key_grad = jnp.einsum("td,te->de", hidden, d_keys, preferred_element_type=jnp.float32)
    value_grad = jnp.einsum("td,te->de", hidden, d_values, preferred_element_type=jnp.float32)
    d_hidden = jnp.dot(d_query, w_query.T, preferred_element_type=jnp.float32)
    d_hidden = d_hidden + jnp.dot(d_keys, w_key.T, preferred_element_type=jnp.float32)
    d_hidden = d_hidden + jnp.dot(d_values, w_value.T, preferred_element_type=jnp.float32)
    d_norm_one, gain_one_grad = pull_one(d_hidden)
    row_grad = d_middle + d_norm_one
    bias_grad = jnp.sum(bias_parts, axis=0).T
    outgoing = (
        jnp.zeros((owners * capacity, model_width), jnp.float32)
        .at[slot_index]
        .set(row_grad)
        .reshape(owners, capacity, model_width)
    )
    arrived = lax.all_to_all(
        outgoing.astype(jnp.bfloat16), "vocab", split_axis=0, concat_axis=0, tiled=True
    ).astype(outgoing.dtype)
    target = jnp.where(asked_ids >= 0, asked_ids - base_row, shard_rows).reshape(-1)
    table_part = (
        jnp.zeros((shard_rows, model_width), jnp.float32)
        .at[target]
        .add(arrived.reshape(-1, model_width), mode="drop")
    )
    table_grad = lax.psum(table_part.astype(jnp.bfloat16), "dp").astype(jnp.float32)
    partial_sums = (
        lax.psum_scatter(query_grad, "vocab", scatter_dimension=1, tiled=True),
        lax.psum_scatter(key_grad, "vocab", scatter_dimension=1, tiled=True),
        lax.psum_scatter(value_grad, "vocab", scatter_dimension=1, tiled=True),
        lax.psum_scatter(out_grad, "vocab", scatter_dimension=1, tiled=True),
        lax.psum_scatter(in_grad, "vocab", scatter_dimension=1, tiled=True),
        lax.psum_scatter(down_grad, "vocab", scatter_dimension=1, tiled=True),
    )
    shares = (
        lax.psum_scatter(
            partial_sums[0].astype(jnp.bfloat16), "dp", scatter_dimension=0, tiled=True
        ).astype(jnp.float32),
        lax.psum_scatter(
            partial_sums[1].astype(jnp.bfloat16), "dp", scatter_dimension=0, tiled=True
        ).astype(jnp.float32),
        lax.psum_scatter(
            partial_sums[2].astype(jnp.bfloat16), "dp", scatter_dimension=0, tiled=True
        ).astype(jnp.float32),
        lax.psum_scatter(
            partial_sums[3].astype(jnp.bfloat16), "dp", scatter_dimension=0, tiled=True
        ).astype(jnp.float32),
        lax.psum_scatter(
            partial_sums[4].astype(jnp.bfloat16), "dp", scatter_dimension=0, tiled=True
        ).astype(jnp.float32),
        lax.psum_scatter(
            partial_sums[5].astype(jnp.bfloat16), "dp", scatter_dimension=0, tiled=True
        ).astype(jnp.float32),
    )
    gain_one_grad, gain_two_grad, bias_grad = lax.psum(
        (gain_one_grad, gain_two_grad, bias_grad), ("dp", "vocab")
    )
    return (
        mixed_out,
        row_grad,
        table_grad,
        gain_one_grad,
        shares[0],
        shares[1],
        shares[2],
        shares[3],
        gain_two_grad,
        shares[4],
        shares[5],
        bias_grad,
    )


def solution(mesh):
    placed = (
        P(("dp", "vocab")),
        P(("dp", "vocab")),
        P("vocab", None),
        P(),
        P(),
        P(),
        P(),
        P(),
        P(),
        P(),
        P(),
        P(),
        P(("dp", "vocab"), None),
    )
    return jax.shard_map(
        body,
        mesh=mesh,
        in_specs=placed,
        out_specs=(
            P(("dp", "vocab"), None),
            P(("dp", "vocab"), None),
            P("vocab", None),
            P(),
            P("dp", "vocab"),
            P("dp", "vocab"),
            P("dp", "vocab"),
            P("dp", "vocab"),
            P(),
            P("dp", "vocab"),
            P("dp", "vocab"),
            P(),
        ),
        check_vma=False,
    )
```

profile of v0, /device:TPU:0, one launch (start us, length us, event | category | flops | bytes accessed | tf_op | source)
XLA Modules:
  0.0 1166.2 jit_solution(2332734033123844742)
XLA Ops:
  26.3 13.6 %gather_fusion = bf16[2048,768]{1,0:T(8,128)(2,1)} fusion(bf16[4016,768]{1,0:T(8,128)(2,1)} %param.19, s32[2048]{0:T(1024)S(1)} %broadcast_clamp_fusion), kind=kCustom, calls=%fused_computation | custom fusion | bytes 6299648 | tf_op jit(solution)/shard_map/jit(_take)/gather | solution.py:124
  60.2 19.1 %copy.186 = f32[2,8,512,512]{3,2,1,0:T(8,128)} copy(f32[2,8,512,512]{3,1,2,0:T(8,128)S(1)} %bitcast.213) | data formatting | bytes 33554432
  90.0 13.0 %copy.140 = f32[12,512,512]{1,2,0:T(8,128)} copy(f32[12,512,512]{2,1,0:T(8,128)} %slice.4) | data formatting | bytes 25165824 | tf_op jit(solution)/shard_map/while | solution.py:138
  102.9 17.1 %all-to-all-done.1 = bf16[8,256,768]{2,1,0:T(8,128)(2,1)} async-done(((bf16[8,256,768]{2,1,0:T(8,128)(2,1)}), bf16[8,256,768]{2,1,0:T(8,128)(2,1)}, u32[]{:S(2)}, u32[]{:S(2)}) %all-to-all-start.1) | async-done | bytes 3145760 | tf_op jit(solution)/shard_map/all_to_all | solution.py:126
  168.4 25.1 %while.29 = (s32[]{:T(128)}, bf16[2,512,12,64]{1,3,2,0:T(8,128)(2,1)}, f32[2,12,512]{2,1,0:T(8,128)S(1)}, bf16[2,512,12,64]{1,3,2,0:T(8,128)(2,1)}, s32[2]{0:T(1...) while((s32[]{:T(128)}, ...), condition=%wide.region_6.7_spmd, body=%wide.region_3.6_spmd.sunk | while | flops 830859776 | bytes 60009620 | solution.py:138
  204.3 18.6 %fusion.85 = bf16[1024,3072]{1,0:T(8,128)(2,1)} fusion(f32[1024,3072]{1,0:T(8,128)S(1)} %fusion.117, bf16[1024,768]{1,0:T(8,128)(2,1)} %param.29, bf16[3072,768]{1,0:T(8,128)(2,1)} %param.27), kind=kOutput, calls=%fused_computation.81 | convolution fusion | flops 4894752768 | bytes 25165824 | tf_op jit(solution)/shard_map/dot_general | solution.py:152
  256.3 232.8 %while.30 = (s32[]{:T(128)}, bf16[2,512,12,64]{1,3,2,0:T(8,128)(2,1)}, bf16[2,512,12,64]{1,3,2,0:T(8,128)(2,1)}, bf16[2,512,12,64]{1,3,2,0:T(8,128)(2,1)}, f32[2...) while((s32[]{:T(128)}, ...), condition=%wide.region_11.12_spmd.clone, body=%wide.region_9.11_spmd.clone.sunk | while | flops 3270633984 | bytes 369768832 | solution.py:164
  265.7 14.2 %multiply_reduce_fusion.5 = (f32[12,512]{1,0:T(8,128)S(1)}, f32[12,512,512]{1,2,0:T(8,128)}) fusion(f32[12,512,512]{1,2,0:T(8,128)} %fusion.190, f32[12,512]{1,0:T(8,128)S(1)} %dynamic-slice_bitcast_fusion.2, f32[12,512,512]{1,2,0:T(8,128)} %get-tuple-element.552, bf16[2,512,12,64]{1,3,2,0:T(8,128)(2,1)S(1)} %copy-done.5, s32[]{:T(128)S(6)} %copy.228, ...), kind=kOutput, calls=%fused_computation.29.clone.1 | convolution fusion | flops 418375680 | bytes 39380480 | tf_op jit(solution)/shard_map/while/body/eval_jaxpr/qhe,khe->hqk/dot_general | solution.py:37
  327.8 15.3 %copy.207 = f32[2,8,512,512]{3,1,2,0:T(8,128)S(1)} copy(f32[2,8,512,512]{3,2,1,0:T(8,128)} %bitcast.212) | data formatting | bytes 33554432 | tf_op jit(solution)/shard_map/while
  343.2 29.7 %fusion.194 = f32[2,12,32]{2,1,0:T(8,128)S(1)} fusion(f32[2,12,32]{2,1,0:T(8,128)S(1)} %get-tuple-element.533, s32[]{:T(128)S(6)} %copy.228, f32[12,262144]{1,0:T(8,128)S(1)} %bitcast.211, s32[262144]{0:T(1024)S(1)} %copy-done.8), kind=kOutput, calls=%fused_computation.47.clone.1 | convolution fusion | flops 1224736768 | bytes 17833988 | tf_op jit(solution)/shard_map/while/body/eval_jaxpr/hn,bn->hb/dot_general | solution.py:70
  382.1 13.7 %multiply_reduce_fusion.5 = (f32[12,512]{1,0:T(8,128)S(1)}, f32[12,512,512]{1,2,0:T(8,128)}) fusion(f32[12,512,512]{1,2,0:T(8,128)} %fusion.190, f32[12,512]{1,0:T(8,128)S(1)} %dynamic-slice_bitcast_fusion.2, f32[12,512,512]{1,2,0:T(8,128)} %get-tuple-element.552, bf16[2,512,12,64]{1,3,2,0:T(8,128)(2,1)S(1)} %copy-done.5, s32[]{:T(128)S(6)} %copy.228, ...), kind=kOutput, calls=%fused_computation.29.clone.1 | convolution fusion | flops 418375680 | bytes 39380480 | tf_op jit(solution)/shard_map/while/body/eval_jaxpr/qhe,khe->hqk/dot_general | solution.py:37
  443.7 15.3 %copy.207 = f32[2,8,512,512]{3,1,2,0:T(8,128)S(1)} copy(f32[2,8,512,512]{3,2,1,0:T(8,128)} %bitcast.212) | data formatting | bytes 33554432 | tf_op jit(solution)/shard_map/while
  459.1 29.7 %fusion.194 = f32[2,12,32]{2,1,0:T(8,128)S(1)} fusion(f32[2,12,32]{2,1,0:T(8,128)S(1)} %get-tuple-element.533, s32[]{:T(128)S(6)} %copy.228, f32[12,262144]{1,0:T(8,128)S(1)} %bitcast.211, s32[262144]{0:T(1024)S(1)} %copy-done.8), kind=kOutput, calls=%fused_computation.47.clone.1 | convolution fusion | flops 1224736768 | bytes 17833988 | tf_op jit(solution)/shard_map/while/body/eval_jaxpr/hn,bn->hb/dot_general | solution.py:70
  571.8 64.8 %reduce-scatter.21.cloned.1.call-done = f32[768,96]{0,1:T(8,128)} async-done(((f32[768,768]{0,1:T(8,128)}), f32[768,96]{0,1:T(8,128)}) %reduce-scatter.21.cloned.1.call-update) | async-done | bytes 294928 | tf_op jit(solution)/shard_map/reduce_scatter | solution.py:197
  638.5 21.0 %all-to-all-done.2 = bf16[8,256,768]{2,1,0:T(8,128)(2,1)} async-done(((bf16[8,256,768]{2,1,0:T(8,128)(2,1)}), bf16[8,256,768]{2,1,0:T(8,128)(2,1)}, u32[]{:S(2)}, u32[]{:S(2)}) %all-to-all-start.2) | async-done | bytes 3145760 | tf_op jit(solution)/shard_map/all_to_all | solution.py:186
  659.5 20.4 %scatter_custom_fusion.2 = f32[4016,768]{1,0:T(8,128)} fusion(s32[2048]{0:T(1024)S(1)} %bitcast.236, bf16[2048,768]{1,0:T(8,128)(2,1)} %bitcast.36, f32[]{:T(128)} %constant.55.clone.1), kind=kCustom, calls=%fused_computation.83 | custom fusion | flops 3145728 | bytes 15482884 | tf_op jit(solution)/shard_map/scatter-add | solution.py:193
  687.8 66.8 %reduce-scatter.33.cloned.1.call-done = f32[3072,96]{0,1:T(8,128)} async-done(((f32[3072,768]{0,1:T(8,128)}), f32[3072,96]{0,1:T(8,128)}) %reduce-scatter.33.cloned.1.call-update) | async-done | bytes 1179664 | tf_op jit(solution)/shard_map/reduce_scatter | solution.py:202
  756.8 97.8 %reduce-scatter.29.cloned.1.call-done = f32[768,384]{1,0:T(8,128)} async-done(((f32[768,3072]{1,0:T(8,128)}), f32[768,384]{1,0:T(8,128)}) %reduce-scatter.29.cloned.1.call-update) | async-done | bytes 1179664 | tf_op jit(solution)/shard_map/reduce_scatter | solution.py:201
  869.2 38.0 %all-reduce = (f32[768]{0:T(1024)}, f32[768]{0:T(1024)}, f32[32,12]{0,1:T(8,128)}) all-reduce(f32[768]{0:T(1024)S(1)} %get-tuple-element.294, f32[768]{0:T(1024)S(1)} %copy-done.42, f32[32,12]{0,1:T(8,128)S(1)} %bitcast.233), channel_id=1, replica_groups=mesh['dp'=4,'vocab'=8] {'dp','vocab'}, use_global_device_ids=true, to_apply=%region_17.18 | all-reduce | flops 1920 | bytes 15360 | tf_op jit(solution)/shard_map/psum | solution.py:224
  910.5 23.3 %reduce-scatter.39.cloned.1.call-done = bf16[192,96]{1,0:T(8,128)(2,1)} async-done(((bf16[768,96]{1,0:T(8,128)(2,1)}), bf16[192,96]{1,0:T(8,128)(2,1)}) %reduce-scatter.39.cloned.1.call-update) | async-done | bytes 36880
  935.5 25.6 %reduce-scatter.37.cloned.1.call-done = bf16[192,96]{1,0:T(8,128)(2,1)} async-done(((bf16[768,96]{1,0:T(8,128)(2,1)}), bf16[192,96]{1,0:T(8,128)(2,1)}) %reduce-scatter.37.cloned.1.call-update) | async-done | bytes 36880
  962.7 138.4 %all-reduce.3.cloned.1.call-done = bf16[4016,768]{1,0:T(8,128)(2,1)} async-done(((bf16[4016,768]{1,0:T(8,128)(2,1)}), bf16[4016,768]{1,0:T(8,128)(2,1)}) %all-reduce.3.cloned.1.call-update) | async-done | bytes 6168592 | tf_op jit(solution)/shard_map/psum | solution.py:195
  1109.5 20.0 %reduce-scatter.35.cloned.1.call-done = bf16[768,96]{0,1:T(8,128)(2,1)} async-done(((bf16[3072,96]{0,1:T(8,128)(2,1)}), bf16[768,96]{0,1:T(8,128)(2,1)}) %reduce-scatter.35.cloned.1.call-update) | async-done | bytes 147472 | tf_op jit(solution)/shard_map/reduce_scatter | solution.py:220
  1131.2 26.6 %reduce-scatter.31.cloned.1.call-done = bf16[192,384]{1,0:T(8,128)(2,1)} async-done(((bf16[768,384]{1,0:T(8,128)(2,1)}), bf16[192,384]{1,0:T(8,128)(2,1)}) %reduce-scatter.31.cloned.1.call-update) | async-done | bytes 147472 | tf_op jit(solution)/shard_map/reduce_scatter | solution.py:217
  (282 shorter events, 408.1 us)
Async XLA Ops:
  7.2 147.8 %copy-start = (bf16[768,768]{1,0:T(8,128)(2,1)S(1)}, bf16[768,768]{1,0:T(8,128)(2,1)}, u32[]{:S(2)}) copy-start(bf16[768,768]{1,0:T(8,128)(2,1)} %param.23) | copy-start | bytes 3538948
  14.2 12.0 %all-to-all-start = ((s32[8,1,256]{2,1,0:T(1,128)}), s32[8,1,256]{2,1,0:T(1,128)S(1)}, u32[]{:S(2)}, u32[]{:S(2)}) async-start(s32[8,1,256]{2,1,0:T(1,128)} %bitcast.7), calls=%async_computation | async-start | bytes 16384 | tf_op jit(solution)/shard_map/all_to_all | solution.py:120
  43.3 76.7 %all-to-all-start.1 = ((bf16[8,256,768]{2,1,0:T(8,128)(2,1)}), bf16[8,256,768]{2,1,0:T(8,128)(2,1)}, u32[]{:S(2)}, u32[]{:S(2)}) async-start(bf16[8,256,768]{2,1,0:T(8,128)(2,1)} %select_select_fusion), calls=%async_computation.1 | async-start | bytes 6291456 | tf_op jit(solution)/shard_map/all_to_all | solution.py:126
  48.4 517.4 %reduce-scatter.27.cloned.1.call-start = ((), (), s32[]{:S(2)}) async-start(), calls=%async_computation.19 | async-start | bytes 2654208 | tf_op jit(solution)/shard_map/reduce_scatter | solution.py:200
  130.1 25.0 %copy-start.33 = (f32[1024]{0:T(1024)}, f32[1024]{0:T(1024)S(1)}, u32[]{:S(2)}) copy-start(f32[1024]{0:T(1024)S(1)} %fusion.114) | copy-start | bytes 12292
  198.9 33.8 %copy-start.16 = (f32[1024,768]{0,1:T(8,128)}, f32[1024,768]{0,1:T(8,128)S(1)}, u32[]{:S(2)}) copy-start(f32[1024,768]{0,1:T(8,128)S(1)} %get-tuple-element.348) | copy-start | bytes 9437188
  198.9 33.8 %copy-start.27 = (f32[1024]{0:T(1024)}, f32[1024]{0:T(1024)S(1)}, u32[]{:S(2)}) copy-start(f32[1024]{0:T(1024)S(1)} %fusion.115) | copy-start | bytes 12292
  204.3 18.7 %copy-start.15 = (f32[1024,3072]{1,0:T(8,128)}, f32[1024,3072]{1,0:T(8,128)S(1)}, u32[]{:S(2)}) copy-start(f32[1024,3072]{1,0:T(8,128)S(1)} %fusion.117) | copy-start | bytes 37748740
  242.9 324.9 %reduce-scatter.25.cloned.1.call-start = ((), (), s32[]{:S(2)}) async-start(), calls=%async_computation.18 | async-start | bytes 2654208 | tf_op jit(solution)/shard_map/reduce_scatter | solution.py:199
  327.8 15.3 %copy-start.8 = (s32[262144]{0:T(1024)S(1)}, s32[262144]{0:T(1024)}, u32[]{:S(2)}) copy-start(s32[262144]{0:T(1024)} %get-tuple-element.556) | copy-start | bytes 3145732 | tf_op jit(solution)/shard_map/while
  343.2 29.7 %copy-start.4 = (bf16[2,512,12,64]{1,3,2,0:T(8,128)(2,1)S(1)}, bf16[2,512,12,64]{1,3,2,0:T(8,128)(2,1)}, u32[]{:S(2)}) copy-start(bf16[2,512,12,64]{1,3,2,0:T(8,128)(2,1)} %copy-done.3) | copy-start | bytes 4718596 | tf_op jit(solution)/shard_map/while
  459.1 29.7 %copy-start.4 = (bf16[2,512,12,64]{1,3,2,0:T(8,128)(2,1)S(1)}, bf16[2,512,12,64]{1,3,2,0:T(8,128)(2,1)}, u32[]{:S(2)}) copy-start(bf16[2,512,12,64]{1,3,2,0:T(8,128)(2,1)} %copy-done.3) | copy-start | bytes 4718596 | tf_op jit(solution)/shard_map/while
  496.8 73.0 %reduce-scatter.23.cloned.1.call-start = ((), (), s32[]{:S(2)}) async-start(), calls=%async_computation.17 | async-start | bytes 2654208 | tf_op jit(solution)/shard_map/reduce_scatter | solution.py:198
  504.5 132.1 %reduce-scatter.21.cloned.1.call-start = ((), (), s32[]{:S(2)}) async-start(), calls=%async_computation.16 | async-start | bytes 2654208 | tf_op jit(solution)/shard_map/reduce_scatter | solution.py:197
  512.1 242.5 %reduce-scatter.33.cloned.1.call-start = ((), (), s32[]{:S(2)}) async-start(), calls=%async_computation.22 | async-start | bytes 10616832 | tf_op jit(solution)/shard_map/reduce_scatter | solution.py:202
  523.6 331.0 %reduce-scatter.29.cloned.1.call-start = ((), (), s32[]{:S(2)}) async-start(), calls=%async_computation.20 | async-start | bytes 10616832 | tf_op jit(solution)/shard_map/reduce_scatter | solution.py:201
  561.2 98.3 %all-to-all-start.2 = ((bf16[8,256,768]{2,1,0:T(8,128)(2,1)}), bf16[8,256,768]{2,1,0:T(8,128)(2,1)}, u32[]{:S(2)}, u32[]{:S(2)}) async-start(bf16[8,256,768]{2,1,0:T(8,128)(2,1)} %bitcast.215), calls=%async_computation.2 | async-start | bytes 6291456 | tf_op jit(solution)/shard_map/all_to_all | solution.py:186
  565.8 341.4 %reduce-scatter.43.cloned.1.call-start = ((), (), s32[]{:S(2)}) async-start(), calls=%async_computation.27 | async-start | bytes 245760
  567.7 341.2 %reduce-scatter.41.cloned.1.call-start = ((), (), s32[]{:S(2)}) async-start(), calls=%async_computation.26 | async-start | bytes 245760
  569.6 364.3 %reduce-scatter.39.cloned.1.call-start = ((), (), s32[]{:S(2)}) async-start(), calls=%async_computation.25 | async-start | bytes 245760
  571.7 389.3 %reduce-scatter.37.cloned.1.call-start = ((), (), s32[]{:S(2)}) async-start(), calls=%async_computation.24 | async-start | bytes 245760
  638.4 462.7 %all-reduce.3.cloned.1.call-start = ((), (), s32[]{:S(2)}) async-start(), calls=%async_computation.15 | async-start | bytes 12337152 | tf_op jit(solution)/shard_map/psum | solution.py:195
  687.7 441.8 %reduce-scatter.35.cloned.1.call-start = ((), (), s32[]{:S(2)}) async-start(), calls=%async_computation.23 | async-start | bytes 737280 | tf_op jit(solution)/shard_map/reduce_scatter | solution.py:220
  756.8 401.0 %reduce-scatter.31.cloned.1.call-start = ((), (), s32[]{:S(2)}) async-start(), calls=%async_computation.21 | async-start | bytes 737280 | tf_op jit(solution)/shard_map/reduce_scatter | solution.py:217
  (49 other events, 242.5 us)
Sparse Core Ops, SparseCore 0:
  243.0 35.1 reduce-scatter.26
  497.0 35.1 reduce-scatter.24
  534.5 35.3 reduce-scatter.22
  572.1 64.4 reduce-scatter.20
  638.7 115.7 reduce-scatter.32
  756.7 97.8 reduce-scatter.28
  857.4 22.3 reduce-scatter.42
  882.5 23.9 reduce-scatter.40
  909.9 23.9 reduce-scatter.38
  937.0 23.9 reduce-scatter.36
  964.5 136.6 all-reduce.2
  1103.8 25.6 reduce-scatter.34
  1132.7 25.0 reduce-scatter.30
where the time goes:
time: 1170 us
  waiting for transfers between devices  502 us (43%)
  matrix products  256 us (22%)
  local copies, waits for them, and re-layouts  248 us (21%)
  other arithmetic  89.4 us (8%)
  blocking collectives  38 us (3%)
  starting transfers between devices  16.6 us (1%)
  between operations  14.9 us (1%)
    psum x1, waiting for transfers between devices, body(): lax.psum(table_part.astype(jnp.bfloat16), 'dp').astype(jnp.float32)  138 us
    reduce_scatter x1, waiting for transfers between devices, body(): lax.psum_scatter(in_grad, 'vocab', scatter_dimension=1, tiled=True)  97.8 us
    reduce_scatter x1, waiting for transfers between devices, body(): lax.psum_scatter(down_grad, 'vocab', scatter_dimension=1, tiled=True)  66.8 us
    reduce_scatter x1, waiting for transfers between devices, body(): lax.psum_scatter(query_grad, 'vocab', scatter_dimension=1, tiled=True)  64.8 us
    while x36, local copies, waits for them, and re-layouts  59.5 us
    dot_general x2, matrix products, attend_backward(): jnp.einsum('hn,bn->hb', d_scores.reshape(head_count, -1), onehot, precisi...  59.3 us
    unnamed x107, local copies, waits for them, and re-layouts  49.2 us
    unnamed x17, waiting for transfers between devices  49.1 us
  transfers between devices with their start and end apart: 16, of which 11 were waited for; matrix products, arithmetic and copies ran while one was open for 38% of the time, Pallas kernels for 0%

commit v1 on v0

v1 whole, which is shorter than its diff:
```python
from functools import partial

import jax
import jax.numpy as jnp
import numpy as np
from jax import lax
from jax.experimental import pallas as pl
from jax.experimental.pallas import tpu as pltpu
from jax.sharding import PartitionSpec as P

EPS = 1e-06
PRECISE = lax.Precision.HIGHEST
MASKED = -1e30
THRESHOLDS = (12, 16, 23, 32, 46, 64, 91)
LANES = 128
NOWHERE = 1 << 30
BF = jnp.bfloat16
F32 = jnp.float32
NN = (((1,), (0,)), ((), ()))
NT = (((1,), (1,)), ((), ()))
TN = (((0,), (0,)), ((), ()))


def mm(left, right, dims=NN):
    return lax.dot_general(left, right, dims, preferred_element_type=F32)


def params(**more):
    return pltpu.CompilerParams(vmem_limit_bytes=56 << 20, **more)


def cost(macs, moved):
    return pl.CostEstimate(flops=2 * macs, bytes_accessed=moved, transcendentals=0)


def whole(shape):
    return pl.BlockSpec(shape, lambda *_: (0,) * len(shape), pipeline_mode=pl.Buffered(1))


def bucket_of(offset):
    distance = np.abs(offset)
    far = 8 + sum((distance >= t).astype(np.int32) for t in THRESHOLDS)
    return np.where(offset > 0, 16, 0) + np.where(distance < 8, distance, far)


def band_offsets():
    lane = np.arange(4 * LANES)
    return np.where(lane < 3 * LANES, lane, lane - 4 * LANES) - LANES


def band_onehot(buckets):
    return (bucket_of(band_offsets())[:, None] == np.arange(buckets)[None, :]).astype(np.float32)


def route_kernel(me_ref, ids_row_ref, ids_col_ref, slot_row_ref, slot_col_ref, ask_ref, *, seq_len, opening, shard, owners, cap, width):
    me = me_ref[0]
    tokens = ids_row_ref.shape[1]
    ids_row, ids_col = ids_row_ref[...], ids_col_ref[...]
    owner_row, owner_col = jnp.zeros_like(ids_row), jnp.zeros_like(ids_col)
    for o in range(1, owners):
        owner_row += (ids_row >= o * shard).astype(jnp.int32)
        owner_col += (ids_col >= o * shard).astype(jnp.int32)

    def places(shape, axis):
        t = lax.broadcasted_iota(jnp.int32, shape, axis)
        within = lax.rem(t, seq_len)
        repeated = (within < opening) & (t >= seq_len)
        return t, jnp.where(within < opening, within, t), jnp.logical_not(repeated)

    t_row, at_row, first_row = places((1, tokens), 1)
    t_col, at_col, first_col = places((tokens, 1), 0)
    key_row = jnp.where(first_row, owner_row, -1)
    key_col = jnp.where(first_col, owner_col, -1)
    rank_col = jnp.sum(((key_row == owner_col) & (t_row < at_col)).astype(jnp.int32), axis=1, keepdims=True)
    rank_row = jnp.sum(((key_col == owner_row) & (t_col < at_row)).astype(jnp.int32), axis=0, keepdims=True)
    slot_row_ref[...] = jnp.where(rank_row < cap, (owner_row ^ me) * cap + rank_row, NOWHERE)
    slot_col_ref[...] = jnp.where(rank_col < cap, (owner_col ^ me) * cap + rank_col, NOWHERE)
    over = (jnp.max(rank_row) >= cap).astype(jnp.int32)
    place_col = jnp.where(first_col & (rank_col < cap), owner_col * width + rank_col, -1)
    step = 4 * LANES
    for start in range(0, owners * width, step):
        lane = lax.broadcasted_iota(jnp.int32, (1, step), 1) + start
        asked = jnp.sum(jnp.where(place_col == lane, ids_col + 1, 0), axis=0, keepdims=True) - 1
        ask_ref[:, start : start + step] = jnp.where(lax.rem(lane, width) == width - 1, over, asked)


def route(token_ids, me, seq_len, opening, shard, owners, cap, width):
    tokens = token_ids.shape[0]
    body = partial(route_kernel, seq_len=seq_len, opening=opening, shard=shard, owners=owners, cap=cap, width=width)
    return pl.pallas_call(
        body,
        in_specs=[pl.BlockSpec(memory_space=pltpu.SMEM), pl.BlockSpec(memory_space=pltpu.VMEM), pl.BlockSpec(memory_space=pltpu.VMEM)],
        out_shape=[
            jax.ShapeDtypeStruct((1, tokens), jnp.int32),
            jax.ShapeDtypeStruct((tokens, 1), jnp.int32),
            jax.ShapeDtypeStruct((1, owners * width), jnp.int32),
        ],
        compiler_params=params(),
        name="route",
    )(me, token_ids.reshape(1, -1), token_ids.reshape(-1, 1))


def project_kernel(slot_ref, rows_refs, gain_ref, wq_ref, wk_ref, wv_ref, x_ref, hidden_ref, q_ref, k_ref, v_ref):
    slot = slot_ref[...]
    x = None
    start = 0
    for rows_ref in rows_refs:
        lane = lax.broadcasted_iota(jnp.int32, (slot.shape[0], rows_ref.shape[0]), 1) + start
        part = mm((lane == slot).astype(F32).astype(BF), rows_ref[...])
        x = part if x is None else x + part
        start += rows_ref.shape[0]
    x_ref[...] = x.astype(BF)
    scale = lax.rsqrt(jnp.mean(x * x, axis=1, keepdims=True) + EPS)
    hidden = (x * scale * gain_ref[...]).astype(BF)
    hidden_ref[...] = hidden
    q_ref[...] = mm(hidden, wq_ref[...]).astype(BF)
    k_ref[...] = mm(hidden, wk_ref[...]).astype(BF)
    v_ref[...] = mm(hidden, wv_ref[...]).astype(BF)


def project(slot_col, rows, gain, w_query, w_key, w_value):
    tokens, width = slot_col.shape[0], gain.shape[1]
    tile = min(256, tokens)
    out = pl.BlockSpec((tile, width), lambda t: (t, 0))
    count = sum(r.shape[0] for r in rows)
    return pl.pallas_call(
        project_kernel,
        grid=(tokens // tile,),
        in_specs=[pl.BlockSpec((tile, 1), lambda t: (t, 0)), [whole(r.shape) for r in rows], whole(gain.shape)]
        + [whole(w_query.shape)] * 3,
        out_specs=[out] * 5,
        out_shape=[jax.ShapeDtypeStruct((tokens, width), BF)] * 5,
        compiler_params=params(),
        cost_estimate=cost(tokens * width * (3 * width + count), 14 * tokens * width),
        name="project",
    )(slot_col, rows, gain, w_query, w_key, w_value)


def band_kernel(line_ref, band_ref):
    line = jnp.broadcast_to(line_ref[0], (LANES, line_ref.shape[2]))
    band_ref[0] = pltpu.roll(line, 0, 1, stride=1, stride_axis=0)[:, : 3 * LANES]


def make_band(rel_bias):
    heads = rel_bias.shape[1]
    line = jnp.dot(band_onehot(rel_bias.shape[0]), rel_bias, precision=PRECISE).T.reshape(heads, 1, -1)
    return pl.pallas_call(
        band_kernel,
        grid=(heads,),
        in_specs=[pl.BlockSpec((1,) + line.shape[1:], lambda h: (h, 0, 0))],
        out_specs=pl.BlockSpec((1, LANES, 3 * LANES), lambda h: (h, 0, 0)),
        out_shape=jax.ShapeDtypeStruct((heads, LANES, 3 * LANES), F32),
        compiler_params=params(),
        name="band",
    )(line)


def attend_kernel(len_ref, far_ref, q_ref, k_ref, v_ref, band_ref, ctx_ref, p_ref):
    pair = pl.program_id(1)
    q, k, v = q_ref[...], k_ref[...], v_ref[...]
    seq_len = q.shape[0]
    blocks = seq_len // LANES
    last = far_ref.shape[0] // 2 - 1
    half = lax.broadcasted_iota(jnp.int32, (1, LANES), 1) // (LANES // 2)
    key_at = lax.broadcasted_iota(jnp.int32, (1, seq_len), 1)
    mask = jnp.where(key_at < len_ref[pl.program_id(0)], 0.0, MASKED)
    none = jnp.zeros((), BF)
    ctx = jnp.zeros((seq_len, LANES), F32)
    for h in range(2):
        k_own, v_own = jnp.where(half == h, k, none), jnp.where(half == h, v, none)
        left, right = far_ref[last, 2 * pair + h], far_ref[2 * last + 1, 2 * pair + h]
        for i in range(blocks):
            raw = mm(q[i * LANES : (i + 1) * LANES], k_own, NT)
            tiles = []
            for j in range(blocks):
                cols = slice(j * LANES, (j + 1) * LANES)
                d = j - i
                if abs(d) <= 1:
                    tiles.append(raw[:, cols] + band_ref[h, :, (d + 1) * LANES : (d + 2) * LANES] + mask[:, cols])
                else:
                    tiles.append(raw[:, cols] + (mask[:, cols] + (left if d < 0 else right)))
            scores = jnp.concatenate(tiles, axis=1)
            grown = jnp.exp(scores - jnp.max(scores, axis=1, keepdims=True))
            total = jnp.sum(grown, axis=1, keepdims=True)
            p_ref[0, h, i * LANES : (i + 1) * LANES, :] = (grown * (1.0 / total)).astype(BF)
        ctx = ctx + mm(p_ref[0, h], v_own)
    ctx_ref[...] = ctx.astype(BF)


def attend(q, k, v, lengths, rel_bias, band):
    seqs, heads = lengths.shape[0], rel_bias.shape[1]
    tokens, width = q.shape
    seq_len = tokens // seqs
    block = pl.BlockSpec((seq_len, LANES), lambda s, p, *_: (s, p))
    return pl.pallas_call(
        attend_kernel,
        grid_spec=pltpu.PrefetchScalarGridSpec(
            num_scalar_prefetch=2,
            grid=(seqs, heads // 2),
            in_specs=[block] * 3 + [pl.BlockSpec((2,) + band.shape[1:], lambda s, p, *_: (p, 0, 0))],
            out_specs=[block, pl.BlockSpec((1, 2, seq_len, seq_len), lambda s, p, *_: (s, p, 0, 0))],
        ),
        out_shape=[
            jax.ShapeDtypeStruct((tokens, width), BF),
            jax.ShapeDtypeStruct((seqs, heads, seq_len, seq_len), BF),
        ],
        compiler_params=params(),
        cost_estimate=cost(tokens * seq_len * width * 8, 2 * tokens * seq_len * heads),
        name="attend",
    )(lengths, rel_bias, q, k, v, band)


def attend_back_kernel(q_ref, k_ref, v_ref, do_ref, p_ref, dq_ref, dk_ref, dv_ref, line_ref, ds_ref, band_ref, far_ref):
    seq_at = pl.program_id(1)
    q, k, v, do = q_ref[...], k_ref[...], v_ref[...], do_ref[...]
    seq_len = q.shape[0]
    blocks = seq_len // LANES
    half = lax.broadcasted_iota(jnp.int32, (1, LANES), 1) // (LANES // 2)
    none = jnp.zeros((), BF)

    @pl.when(seq_at == 0)
    def _():
        band_ref[...] = jnp.zeros_like(band_ref)
        far_ref[...] = jnp.zeros_like(far_ref)

    dq = dk = dv = jnp.zeros((seq_len, LANES), F32)
    for h in range(2):
        k_own, v_own = jnp.where(half == h, k, none), jnp.where(half == h, v, none)
        q_own, do_own = jnp.where(half == h, q, none), jnp.where(half == h, do, none)
        near = [jnp.zeros((LANES, LANES), F32) for _ in range(3)]
        far = [jnp.zeros((8, LANES), F32) for _ in range(2)]
        for i in range(blocks):
            rows = slice(i * LANES, (i + 1) * LANES)
            probs = p_ref[0, h, rows, :].astype(F32)
            weighed = probs * mm(do[rows], v_own, NT)
            ds = weighed - probs * jnp.sum(weighed, axis=1, keepdims=True)
            for j in range(blocks):
                d = j - i
                tile = ds[:, j * LANES : (j + 1) * LANES]
                if abs(d) <= 1:
                    near[d + 1] = near[d + 1] + tile
                else:
                    side = 0 if d < 0 else 1
                    far[side] = far[side] + jnp.sum(tile.reshape(LANES // 8, 8, LANES), axis=0)
            ds_ref[rows, :] = ds.astype(BF)
        for d in range(3):
            band_ref[h, :, d * LANES : (d + 1) * LANES] += near[d]
        for side in range(2):
            far_ref[h, :, side * LANES : (side + 1) * LANES] += far[side]
        d_low = ds_ref[...]
        dk = dk + mm(d_low, q_own, TN)
        dv = dv + mm(p_ref[0, h], do_own, TN)
        dq = dq + mm(d_low, k_own)
    dq_ref[...], dk_ref[...], dv_ref[...] = dq.astype(BF), dk.astype(BF), dv.astype(BF)

    @pl.when(seq_at == pl.num_programs(1) - 1)
    def _():
        row = lax.broadcasted_iota(jnp.int32, (8, 1), 0)
        for h in range(2):
            padded = jnp.concatenate([band_ref[h], jnp.zeros((LANES, LANES), F32)], axis=1)
            turned = padded[:8]
            for start in range(8, LANES, 8):
                turned = turned + pltpu.roll(padded[start : start + 8], 4 * LANES - start, 1)
            for bit in (1, 2, 4):
                turned = jnp.where(row & bit > 0, pltpu.roll(turned, 4 * LANES - bit, 1), turned)
            line_ref[0, h : h + 1, :] = jnp.sum(turned, axis=0, keepdims=True)
            line_ref[0, 2 + h : 3 + h, : 2 * LANES] = jnp.sum(far_ref[h], axis=0, keepdims=True)


def attend_back(q, k, v, d_context, probs):
    seqs, heads, seq_len, _ = probs.shape
    tokens, width = q.shape
    block = pl.BlockSpec((seq_len, LANES), lambda p, s: (s, p))
    dq, dk, dv, lines = pl.pallas_call(
        attend_back_kernel,
        grid=(heads // 2, seqs),
        in_specs=[block] * 4 + [pl.BlockSpec((1, 2, seq_len, seq_len), lambda p, s: (s, p, 0, 0))],
        out_specs=[block] * 3 + [pl.BlockSpec((1, 8, 4 * LANES), lambda p, s: (p, 0, 0))],
        out_shape=[jax.ShapeDtypeStruct((tokens, width), BF)] * 3
        + [jax.ShapeDtypeStruct((heads // 2, 8, 4 * LANES), F32)],
        scratch_shapes=[
            pltpu.VMEM((seq_len, seq_len), BF),
            pltpu.VMEM((2, LANES, 3 * LANES), F32),
            pltpu.VMEM((2, 8, 2 * LANES), F32),
        ],
        compiler_params=params(),
        cost_estimate=cost(tokens * seq_len * width * 12, 2 * tokens * seq_len * heads),
        name="attend_back",
    )(q, k, v, d_context, probs)
    near = lines[:, 0:2, :].reshape(heads, -1)
    far = jnp.sum(lines[:, 2:4, : 2 * LANES].reshape(heads, 2, LANES), axis=2)
    return dq, dk, dv, near, far


def middle_kernel(x_ref, ctx_ref, cot_ref, gain_ref, w_out_ref, w_in_ref, w_down_ref, mixed_ref, act_ref, d_pre_ref, hidden_t_ref, d_mid_ref, d_att_ref, d_ctx_ref, gain_grad_ref, *, chunk):
    mid = x_ref[...].astype(F32) + mm(ctx_ref[...], w_out_ref[...])
    gain = gain_ref[...]
    scale = lax.rsqrt(jnp.mean(mid * mid, axis=1, keepdims=True) + EPS)
    hidden_full = mid * scale * gain
    hidden = hidden_full.astype(BF)
    hidden_t_ref[...] = hidden_full.T.astype(BF)
    cot = cot_ref[...]
    mixed, d_hidden = mid, jnp.zeros_like(mid)
    slope = float(np.sqrt(2 / np.pi))
    for start in range(0, w_in_ref.shape[1], chunk):
        cols = slice(start, start + chunk)
        pre = mm(hidden, w_in_ref[:, cols])
        d_act = mm(cot, w_down_ref[cols, :], NT)
        square = pre * pre
        bent = jnp.tanh(slope * pre * (1.0 + 0.044715 * square))
        open_half = 0.5 + 0.5 * bent
        act = (pre * open_half).astype(BF)
        curve = (0.5 * slope) * pre * (1.0 - bent * bent) * (1.0 + (3 * 0.044715) * square)
        d_pre = (d_act * (open_half + curve)).astype(BF)
        act_ref[:, cols] = act
        d_pre_ref[:, cols] = d_pre
        mixed = mixed + mm(act, w_down_ref[cols, :])
        d_hidden = d_hidden + mm(d_pre, w_in_ref[:, cols], NT)
    mixed_ref[...] = mixed.astype(BF)
    u = d_hidden * gain
    swing = jnp.mean(u * mid, axis=1, keepdims=True)
    d_mid = cot.astype(F32) + scale * u - mid * (scale * scale * scale * swing)
    d_mid_ref[...] = d_mid
    d_att = d_mid.astype(BF)
    d_att_ref[...] = d_att
    d_ctx_ref[...] = mm(d_att, w_out_ref[...], NT).astype(BF)

    @pl.when(pl.program_id(0) == 0)
    def _():
        gain_grad_ref[...] = jnp.zeros_like(gain_grad_ref)

    gain_grad_ref[...] += jnp.sum((d_hidden * mid * scale).reshape(-1, 8, mid.shape[1]), axis=0)


def middle_part(x, ctx, cot, gain, w_out, w_in, w_down):
    tokens, width = x.shape
    wide = w_in.shape[1]
    tile = min(256, tokens)
    rows = pl.BlockSpec((tile, width), lambda t: (t, 0))
    wide_rows = pl.BlockSpec((tile, wide), lambda t: (t, 0))
    return pl.pallas_call(
        partial(middle_kernel, chunk=min(768, wide)),
        grid=(tokens // tile,),
        in_specs=[rows] * 3 + [whole(a.shape) for a in (gain, w_out, w_in, w_down)],
        out_specs=[rows, wide_rows, wide_rows, pl.BlockSpec((width, tile), lambda t: (0, t)), rows, rows, rows]
        + [pl.BlockSpec((8, width), lambda t: (0, 0))],
        out_shape=[
            jax.ShapeDtypeStruct((tokens, width), BF),
            jax.ShapeDtypeStruct((tokens, wide), BF),
            jax.ShapeDtypeStruct((tokens, wide), BF),
            jax.ShapeDtypeStruct((width, tokens), BF),
            jax.ShapeDtypeStruct((tokens, width), F32),
            jax.ShapeDtypeStruct((tokens, width), BF),
            jax.ShapeDtypeStruct((tokens, width), BF),
            jax.ShapeDtypeStruct((8, width), F32),
        ],
        compiler_params=params(),
        cost_estimate=cost(tokens * width * (4 * wide + 2 * width), 4 * width * wide + 8 * tokens * (wide + width)),
        name="middle",
    )(x, ctx, cot, gain, w_out, w_in, w_down)


def wide_grads_kernel(core_ref, hidden_t_ref, cot_t_ref, d_pre_ref, act_ref, in_keep_ref, in_send_ref, down_keep_ref, down_send_ref, parts_ref, *, groups, owners):
    core = core_ref[0]
    step = pl.program_id(0)
    in_part = mm(hidden_t_ref[...], d_pre_ref[...]).astype(BF).reshape(groups, 1, -1, d_pre_ref.shape[1])

    @pl.when(lax.rem(step, 2) == core)
    def _():
        in_keep_ref[...] = in_part

    @pl.when(lax.rem(step, 2) != core)
    def _():
        in_send_ref[...] = in_part

    parts_ref[...] = mm(cot_t_ref[...], act_ref[...]).astype(BF).reshape(parts_ref.shape)
    for z in range(owners // 2):
        down_keep_ref[0, z, 0] = parts_ref[2 * z + core]
        down_send_ref[0, z, 0] = parts_ref[2 * z + 1 - core]


def wide_grads(core, hidden_t, cot_t, d_pre, act, groups, owners):
    width, tokens = hidden_t.shape
    wide = act.shape[1]
    lanes, zs = wide // owners, owners // 2
    cols = pl.BlockSpec((tokens, lanes), lambda v, *_: (0, v))
    in_out = pl.BlockSpec((groups, 1, width // groups, lanes), lambda v, *_: (0, v // 2, 0, 0))
    halves = owners // groups
    down_out = pl.BlockSpec((1, zs, 1, width // owners, lanes), lambda v, *_: (v // halves, 0, v % halves, 0, 0))
    in_shape = jax.ShapeDtypeStruct((groups, zs, width // groups, lanes), BF)
    down_shape = jax.ShapeDtypeStruct((groups, zs, halves, width // owners, lanes), BF)
    return pl.pallas_call(
        partial(wide_grads_kernel, groups=groups, owners=owners),
        grid_spec=pltpu.PrefetchScalarGridSpec(
            num_scalar_prefetch=1,
            grid=(owners,),
            in_specs=[whole(hidden_t.shape), whole(cot_t.shape), cols, cols],
            out_specs=[in_out, in_out, down_out, down_out],
            scratch_shapes=[pltpu.VMEM((owners, width // owners, lanes), BF)],
        ),
        out_shape=[in_shape, in_shape, down_shape, down_shape],
        compiler_params=params(),
        cost_estimate=cost(2 * tokens * width * wide, 4 * wide * (tokens + width)),
        name="wide_grads",
    )(core, hidden_t, cot_t, d_pre, act)


def square_grads_kernel(core_ref, left_refs, right_refs, keep_ref, send_ref, parts_ref, *, groups, owners):
    core = core_ref[0]
    for n, (left_ref, right_ref) in enumerate(zip(left_refs, right_refs)):
        parts_ref[n] = mm(left_ref[...], right_ref[...], TN).astype(BF).reshape(parts_ref.shape[1:])
    lanes = right_refs[0].shape[1] // groups
    for z in range(owners // 2):
        for target_ref, v in ((keep_ref, 2 * z + core), (send_ref, 2 * z + 1 - core)):
            first, second = parts_ref[0, v], parts_ref[1, v]
            for d in range(groups):
                cols = slice(d * lanes, (d + 1) * lanes)
                target_ref[d, z] = jnp.concatenate([first[:, cols], second[:, cols]], axis=1)


def square_grads(core, lefts, rights, groups, owners):
    tokens, width = rights[0].shape
    shape = (groups, owners // 2, width // owners, 2 * width // groups)
    full = [whole((tokens, width))] * 2
    return pl.pallas_call(
        partial(square_grads_kernel, groups=groups, owners=owners),
        in_specs=[pl.BlockSpec(memory_space=pltpu.SMEM), [pl.BlockSpec(memory_space=pltpu.VMEM)] * 2, [pl.BlockSpec(memory_space=pltpu.VMEM)] * 2],
        out_shape=[jax.ShapeDtypeStruct(shape, BF)] * 2,
        scratch_shapes=[pltpu.VMEM((2, owners, width // owners, width), BF)],
        compiler_params=params(),
        cost_estimate=cost(2 * tokens * width * width, 12 * tokens * width),
        name="square_grads",
    )(core, lefts, rights)


def rows_kernel(slot_ref, x_ref, d_mid_ref, dq_ref, dk_ref, dv_ref, gain_ref, wq_ref, wk_ref, wv_ref, row_ref, gain_grad_ref, out_refs, total_ref):
    d_hidden = mm(dq_ref[...], wq_ref[...], NT) + mm(dk_ref[...], wk_ref[...], NT) + mm(dv_ref[...], wv_ref[...], NT)
    x = x_ref[...].astype(F32)
    scale = lax.rsqrt(jnp.mean(x * x, axis=1, keepdims=True) + EPS)
    u = d_hidden * gain_ref[...]
    swing = jnp.mean(u * x, axis=1, keepdims=True)
    row = d_mid_ref[...] + scale * u - x * (scale * scale * scale * swing)
    row_ref[...] = row
    at = pl.program_id(0)

    @pl.when(at == 0)
    def _():
        gain_grad_ref[...] = jnp.zeros_like(gain_grad_ref)
        total_ref[...] = jnp.zeros_like(total_ref)

    gain_grad_ref[...] += jnp.sum((d_hidden * x * scale).reshape(-1, 8, x.shape[1]), axis=0)
    slot = slot_ref[...]
    place = lax.broadcasted_iota(jnp.int32, (total_ref.shape[0], slot.shape[1]), 0)
    total_ref[...] += mm((place == slot).astype(F32).astype(BF), row.astype(BF))

    @pl.when(at == pl.num_programs(0) - 1)
    def _():
        start = 0
        for out_ref in out_refs:
            out_ref[...] = total_ref[start : start + out_ref.shape[0], :].astype(BF)
            start += out_ref.shape[0]


def rows_back(slot_row, x, d_mid, dq, dk, dv, gain, w_query, w_key, w_value, owners, cap):
    tokens, width = x.shape
    tile = min(256, tokens)
    rows = pl.BlockSpec((tile, width), lambda t: (t, 0))
    return pl.pallas_call(
        rows_kernel,
        grid=(tokens // tile,),
        in_specs=[pl.BlockSpec((1, tile), lambda t: (0, t))] + [rows] * 5 + [whole(gain.shape)] + [whole(w_query.shape)] * 3,
        out_specs=[rows, pl.BlockSpec((8, width), lambda t: (0, 0)), [whole((cap, width))] * owners],
        out_shape=[
            jax.ShapeDtypeStruct((tokens, width), F32),
            jax.ShapeDtypeStruct((8, width), F32),
            [jax.ShapeDtypeStruct((cap, width), BF)] * owners,
        ],
        scratch_shapes=[pltpu.VMEM((owners * cap, width), F32)],
        compiler_params=params(),
        cost_estimate=cost(tokens * width * (3 * width + owners * cap), 20 * tokens * width),
        name="rows_back",
    )(slot_row, x, d_mid, dq, dk, dv, gain, w_query, w_key, w_value)


def place_kernel(target_refs, rows_refs, out_ref):
    base = pl.program_id(0) * out_ref.shape[0]
    total = None
    for target_ref, rows_ref in zip(target_refs, rows_refs):
        row = lax.broadcasted_iota(jnp.int32, (out_ref.shape[0], rows_ref.shape[0]), 0) + base
        part = mm((row == target_ref[...]).astype(F32).astype(BF), rows_ref[...])
        total = part if total is None else total + part
    out_ref[...] = total


def place_rows(targets, rows, shard):
    width = rows[0].shape[1]
    tile = min(512, shard)
    count = sum(r.shape[0] for r in rows)
    return pl.pallas_call(
        place_kernel,
        grid=(pl.cdiv(shard, tile),),
        in_specs=[[whole(t.shape) for t in targets], [whole(r.shape) for r in rows]],
        out_specs=pl.BlockSpec((tile, width), lambda t: (t, 0)),
        out_shape=jax.ShapeDtypeStruct((shard, width), F32),
        compiler_params=params(),
        cost_estimate=cost(shard * width * count, 4 * shard * width + 2 * count * width),
        name="place_rows",
    )(targets, rows)


def swap(value, axis, bit):
    count = lax.axis_size(axis)
    return lax.ppermute(value, axis, [(i, i ^ bit) for i in range(count)])


def add_low(first, second):
    return (first.astype(F32) + second.astype(F32)).astype(BF)


def pick(blocks, at):
    return lax.dynamic_index_in_dim(blocks, at, 0, keepdims=False)


def exchange(blocks):
    owners = lax.axis_size("vocab")
    if owners <= 8:
        return [blocks[0]] + [swap(blocks[k], "vocab", k) for k in range(1, owners)]
    order = lax.axis_index("vocab") ^ jnp.arange(owners)
    sent = jnp.take(jnp.stack(blocks), order, axis=0)
    came = lax.all_to_all(sent, "vocab", split_axis=0, concat_axis=0, tiled=True)
    return list(jnp.take(came, order, axis=0))


def gather_dp(block):
    half = block.shape[0] // 2
    by_x, by_y = swap(block, "dp", 1), swap(block, "dp", 2)
    far_low = swap(by_x[:half], "dp", 2)
    far_high = swap(by_y[half:], "dp", 1)
    return [block, by_x, by_y, far_low, far_high]


def reduce_shares(keep, came, first, second):
    place = lax.axis_index("dp")
    bit = {1: place % 2, 2: place // 2}
    part = add_low(keep, came)
    part = part.reshape((2, 2) + part.shape[1:])
    if first == 1:
        part = jnp.moveaxis(part, 1, 0)
    part = add_low(pick(part, bit[first]), swap(pick(part, 1 - bit[first]), "dp", first))
    part = add_low(pick(part, bit[second]), swap(pick(part, 1 - bit[second]), "dp", second))
    z = lax.axis_index("vocab") // 2
    total = pick(part, z).astype(F32)
    for k in range(1, lax.axis_size("vocab") // 2):
        total = total + swap(pick(part, z ^ k), "vocab", 2 * k).astype(F32)
    return total


def sum_all(value):
    for axis in ("vocab", "dp"):
        bit = 1
        while bit < lax.axis_size(axis):
            value = value + swap(value, axis, bit)
            bit *= 2
    return value


def spare_slots(token_ids, seq_len, opening, shard, owners, cap, spare):
    tokens = token_ids.shape[0]
    t = jnp.arange(tokens, dtype=jnp.int32)
    within = t % seq_len
    at = jnp.where(within < opening, within, t)
    first = (within >= opening) | (t < seq_len)
    owner = token_ids // shard
    same = (owner[:, None] == owner[None, :]) & first[None, :] & (t[None, :] < at[:, None])
    rank = jnp.sum(same.astype(jnp.int32), axis=1) - cap
    slot = jnp.where(rank >= 0, owner * spare + rank, owners * spare)
    request = jnp.full((owners * spare + 1,), -1, jnp.int32).at[slot].set(token_ids)[:-1]
    asked = lax.all_to_all(request.reshape(owners, spare), "vocab", split_axis=0, concat_axis=0, tiled=True)
    return slot, asked


def body(
    token_ids,
    seq_lengths,
    table,
    gain_one,
    w_query,
    w_key,
    w_value,
    w_out,
    gain_two,
    w_in,
    w_down,
    rel_bias,
    cotangent,
):
    owners, groups = lax.axis_size("vocab"), lax.axis_size("dp")
    me = lax.axis_index("vocab").astype(jnp.int32)
    core = (me % 2).reshape(1)
    shard, width = table.shape
    tokens, seqs = token_ids.shape[0], seq_lengths.shape[0]
    seq_len = tokens // seqs
    heads = rel_bias.shape[1]
    most = 2 * tokens // owners
    opening = most // seqs
    cap = min(most, -(-(9 * most // 16) // 16) * 16)
    spare = most - cap
    lanes = -(-(cap + 1) // LANES) * LANES
    gain_one_row, gain_two_row = gain_one.reshape(1, -1), gain_two.reshape(1, -1)

    slot_row, slot_col, ask = route(token_ids, me.reshape(1), seq_len, opening, shard, owners, cap, lanes)
    asked = lax.all_to_all(ask.reshape(owners, lanes), "vocab", split_axis=0, concat_axis=0, tiled=True)
    asked = jnp.take(asked, me ^ jnp.arange(owners), axis=0)
    by_x = swap(asked, "dp", 1)
    by_y = swap(jnp.stack([asked, by_x]), "dp", 2)
    asked_all = jnp.stack([asked, by_x, by_y[0], by_y[1]])
    overflow = jnp.max(asked_all[:, :, lanes - 1]) > 0 if spare else None
    base = me * shard
    targets = jnp.where(asked_all[:, :, :cap] >= 0, asked_all[:, :, :cap] - base, -1)
    local = jnp.clip(asked[:, :cap] - base, 0, shard - 1)
    picked = [jnp.take(table, local[k], axis=0, mode="clip") for k in range(owners)]
    rows = exchange(picked)

    band = make_band(rel_bias)
    cot_t = cotangent.T

    def project_plain(*rows_in):
        return project(slot_col, list(rows_in), gain_one_row, w_query, w_key, w_value)

    def spare_rows(args):
        return spare_slots(token_ids, seq_len, opening, shard, owners, cap, spare)

    def project_spare(*rows_in):
        slot, asked_more = spare_rows(None)
        found = jnp.take(table, jnp.clip(asked_more - base, 0, shard - 1), axis=0)
        came = lax.all_to_all(found, "vocab", split_axis=0, concat_axis=0, tiled=True).reshape(-1, width)
        more = jnp.take(came, jnp.clip(slot, 0, owners * spare - 1), axis=0)
        more = jnp.where((slot < owners * spare)[:, None], more, jnp.zeros((), BF))
        marked = jnp.where(slot < owners * spare, owners * cap + jnp.arange(tokens, dtype=jnp.int32), slot_col[:, 0])
        return project(marked[:, None], list(rows_in) + [more], gain_one_row, w_query, w_key, w_value)

    if spare:
        x, hidden, q, k, v = lax.cond(overflow, project_spare, project_plain, *rows)
    else:
        x, hidden, q, k, v = project_plain(*rows)

    ctx, probs = attend(q, k, v, seq_lengths, rel_bias, band)
    mixed_out, act, d_pre, hidden_t, d_mid, d_att, d_ctx, gain_two_part = middle_part(
        x, ctx, cotangent, gain_two_row, w_out, w_in, w_down
    )
    packed = owners == 8 and groups == 4 and (width // groups) % 64 == 0 and (w_in.shape[1] // owners) % LANES == 0
    if packed:
        in_keep, in_send, down_keep, down_send = wide_grads(core, hidden_t, cot_t, d_pre, act, groups, owners)
        in_came, down_came = swap(in_send, "vocab", 1), swap(down_send, "vocab", 1)
        in_share = reduce_shares(in_keep, in_came, 1, 2)
        down_share = reduce_shares(down_keep, down_came, 2, 1)

    dq, dk, dv, near, far = attend_back(q, k, v, d_ctx, probs)
    row_grad, gain_one_part, outgoing = rows_back(
        slot_row, x, d_mid, dq, dk, dv, gain_one_row, w_query, w_key, w_value, owners, cap
    )
    arrived = exchange(outgoing)

    if owners == 8:
        batches = [(0, 2), (2, 4), (4, 6), (6, 8)]
    else:
        batches = [(0, owners)]
    placed_targets, placed_rows = [], []
    for low, high in batches:
        parts = gather_dp(jnp.concatenate(arrived[low:high], axis=0))
        wanted = targets[:, low:high].reshape(groups, 1, -1)
        half = wanted.shape[2] // 2
        placed_rows += parts
        placed_targets += [wanted[0], wanted[1], wanted[2], wanted[3][:, :half], wanted[3][:, half:]]

    def place_plain(*args):
        n = len(args) // 2
        return place_rows(list(args[:n]), list(args[n:]), shard)

    def place_spare(*args):
        slot, asked_more = spare_rows(None)
        sent = jnp.zeros((owners * spare + 1, width), F32).at[slot].add(row_grad)[:-1]
        came = lax.all_to_all(
            sent.astype(BF).reshape(owners, spare, width), "vocab", split_axis=0, concat_axis=0, tiled=True
        )
        target = jnp.where(asked_more >= 0, asked_more - base, shard).reshape(-1)
        part = jnp.zeros((shard, width), F32).at[target].add(came.reshape(-1, width).astype(F32), mode="drop")
        return place_plain(*args) + lax.psum(part, "dp")

    if spare:
        table_grad = lax.cond(overflow, place_spare, place_plain, *placed_targets, *placed_rows)
    else:
        table_grad = place_plain(*placed_targets, *placed_rows)

    if packed:
        qk_keep, qk_send = square_grads(core, [dq, dk], [hidden, hidden], groups, owners)
        vo_keep, vo_send = square_grads(core, [dv, d_att], [hidden, ctx], groups, owners)
        qk_share = reduce_shares(qk_keep, swap(qk_send, "vocab", 1), 1, 2)
        vo_share = reduce_shares(vo_keep, swap(vo_send, "vocab", 1), 2, 1)
        part = width // groups
        query_grad, key_grad = qk_share[:, :part].T, qk_share[:, part:].T
        value_grad, out_grad = vo_share[:, :part].T, vo_share[:, part:].T
        in_grad = in_share
        down_grad = jnp.swapaxes(down_share, 1, 2).reshape(-1, width // owners)
    else:
        def spread(left, right):
            full = jnp.einsum("td,te->de", left, right, preferred_element_type=F32)
            part = lax.psum_scatter(full, "vocab", scatter_dimension=1, tiled=True).astype(BF)
            return lax.psum_scatter(part, "dp", scatter_dimension=0, tiled=True).astype(F32)

        query_grad, key_grad, value_grad = spread(hidden, dq), spread(hidden, dk), spread(hidden, dv)
        out_grad = spread(ctx, d_att)
        in_grad = spread(hidden_t.T, d_pre)
        down_grad = spread(act, cotangent)

    buckets = rel_bias.shape[0]
    bias_part = jnp.dot(near, band_onehot(buckets), precision=PRECISE)
    last = buckets // 2 - 1
    bias_part = bias_part.at[:, last].add(far[:, 0]).at[:, 2 * last + 1].add(far[:, 1])
    small = jnp.concatenate(
        [jnp.sum(gain_one_part, axis=0), jnp.sum(gain_two_part, axis=0), bias_part.T.reshape(-1)]
    )
    small = jnp.pad(small, (0, -small.shape[0] % (8 * LANES))).reshape(-1, LANES)
    small = sum_all(small).reshape(-1)
    gain_one_grad, gain_two_grad = small[:width], small[width : 2 * width]
    bias_grad = small[2 * width : 2 * width + buckets * heads].reshape(buckets, heads)
    return (
        mixed_out,
        row_grad,
        table_grad,
        gain_one_grad,
        query_grad,
        key_grad,
        value_grad,
        out_grad,
        gain_two_grad,
        in_grad,
        down_grad,
        bias_grad,
    )


def solution(mesh):
    spread = ("dp", "vocab")
    placed = (
        P(spread),
        P(spread),
        P("vocab", None),
        P(),
        P(),
        P(),
        P(),
        P(),
        P(),
        P(),
        P(),
        P(),
        P(spread, None),
    )
    return jax.shard_map(
        body,
        mesh=mesh,
        in_specs=placed,
        out_specs=(
            P(spread, None),
            P(spread, None),
            P("vocab", None),
            P(),
            P("dp", "vocab"),
            P("dp", "vocab"),
            P("dp", "vocab"),
            P("dp", "vocab"),
            P(),
            P("dp", "vocab"),
            P("dp", "vocab"),
            P(),
        ),
        check_vma=False,
    )
```

time: 1170 us -> 556 us (0.48)
  waiting for transfers between devices: 502 us -> 125 us
  matrix products: 256 us -> 1.53 us
  Pallas kernels: 0 us -> 211 us
  local copies, waits for them, and re-layouts: 248 us -> 87.1 us
  other arithmetic: 89.4 us -> 19.3 us
  starting transfers between devices: 16.6 us -> 77.4 us
  blocking collectives: 38 us -> 0 us
    reduce_scatter x8 -> x0, waiting for transfers between devices: 276 us -> none  [the longest x1 97.8 us: body(): lax.psum_scatter(in_grad, 'vocab', scatter_dimension=1, tiled=True)]
    dot_general x36 -> x2, matrix products: 256 us -> 1.53 us  [the longest x1 1.29 us: make_band(): jnp.dot(band_onehot(rel_bias.shape[0]), rel_bias, precision=PRECISE)]
    pallas_call x0 -> x11, Pallas kernels: none -> 211 us  [the longest x1 57.4 us: place_rows(): pl.pallas_call(place_kernel, grid=(pl.cdiv(shard, tile),), in_specs=[[who...]
    psum x1 -> x0, waiting for transfers between devices: 138 us -> none  [body(): lax.psum(table_part.astype(jnp.bfloat16), 'dp').astype(jnp.float32)]
    ppermute x0 -> x61, waiting for transfers between devices: none -> 125 us  [swap(): return lax.ppermute(value, axis, [(i, i ^ bit) for i in range(count)])]
    while x44 -> x0, local copies, waits for them, and re-layouts: 92.7 us -> none
    ppermute x0 -> x61, starting transfers between devices: none -> 71.1 us  [swap(): return lax.ppermute(value, axis, [(i, i ^ bit) for i in range(count)])]
    unnamed x17 -> x0, waiting for transfers between devices: 49.1 us -> none
  transfers between devices with their start and end apart: 16 -> 62, of which waited for: 11 -> 26; matrix products, arithmetic and copies ran while one was open for 38% -> 18% of each run, Pallas kernels for 0% -> 18%
where the time goes in v1:
time: 556 us; the launch traced here: 550 us
  Pallas kernels  211 us (38%)
  waiting for transfers between devices  125 us (22%)
  local copies, waits for them, and re-layouts  87.1 us (16%)
  starting transfers between devices  77.4 us (14%)
  other arithmetic  19.3 us (3%)
  between operations  16.3 us (3%)
  loops' own time  12.3 us (2%)
    ppermute x61, waiting for transfers between devices, swap(): return lax.ppermute(value, axis, [(i, i ^ bit) for i in range(count)])  125 us
    ppermute x61, starting transfers between devices, swap(): return lax.ppermute(value, axis, [(i, i ^ bit) for i in range(count)])  71.1 us
    pallas_call x1, Pallas kernels, place_rows(): pl.pallas_call(place_kernel, grid=(pl.cdiv(shard, tile),), in_specs=[[who...  57.4 us
    gather x8, local copies, waits for them, and re-layouts, body(): jnp.take(table, local[k], axis=0, mode='clip')  36.6 us
    pallas_call x1, Pallas kernels, middle_part(): pl.pallas_call(partial(middle_kernel, chunk=min(768, wide)), grid=(tokens...  34.4 us
    pallas_call x1, Pallas kernels, attend_back(): pl.pallas_call(attend_back_kernel, grid=(heads // 2, seqs), in_specs=[blo...  26.5 us
    pallas_call x1, Pallas kernels, wide_grads(): pl.pallas_call(partial(wide_grads_kernel, groups=groups, owners=owners),...  21 us
    pallas_call x1, Pallas kernels, attend(): pl.pallas_call(attend_kernel, grid_spec=pltpu.PrefetchScalarGridSpec(num_...  17.9 us
  transfers between devices with their start and end apart: 62, of which 26 were waited for; matrix products, arithmetic and copies ran while one was open for 18% of the time, Pallas kernels for 18%

profile of v1, /device:TPU:0, one launch (start us, length us, event | category | flops | bytes accessed | tf_op | source)
XLA Modules:
  0.0 550.4 jit_solution(9260961758251421683)
XLA Ops:
  13.0 6.3 %all-to-all-start.4 = ((s32[8,1,256]{2,1,0:T(1,128)}), s32[8,1,256]{2,1,0:T(1,128)S(1)}, u32[]{:S(2)}, u32[]{:S(2)}) async-start(s32[8,1,256]{2,1,0:T(1,128)} %bitcast.176), calls=%async_computation.4 | async-start | bytes 16384 | tf_op jit(solution)/shard_map/all_to_all | solution.py:612
  26.4 6.9 %band.1.band_ref = f32[12,128,384]{2,1,0:T(8,128)} custom-call(f32[12,1,512]{2,1,0:T(1,128)} %reshape.409.line_ref), custom_call_target="tpu_custom_call" | custom-call | tf_op jit(solution)/shard_map/band/pallas_call | solution.py:147
  67.5 4.6 gather_fusion.7
  86.9 5.1 collective-permute-start.6
  92.0 16.8 %collective-permute-done.5 = bf16[144,768]{1,0:T(8,128)(2,1)S(1)} collective-permute-done((bf16[144,768]{1,0:T(8,128)(2,1)S(1)}, bf16[144,768]{1,0:T(8,128)(2,1)S(1)}, u32[]{:S(2)}, u32[]{:S(2)}) %collective-permute-start.5) | collective-permute-done | bytes 221216 | tf_op jit(solution)/shard_map/ppermute | solution.py:513
  108.8 7.8 %collective-permute-done.6 = bf16[144,768]{1,0:T(8,128)(2,1)S(1)} collective-permute-done((bf16[144,768]{1,0:T(8,128)(2,1)S(1)}, bf16[144,768]{1,0:T(8,128)(2,1)S(1)}, u32[]{:S(2)}, u32[]{:S(2)}) %collective-permute-start.6) | collective-permute-done | bytes 221216 | tf_op jit(solution)/shard_map/ppermute | solution.py:513
  120.3 21.3 %conditional.2 = ((bf16[1024,768]{1,0:T(8,128)(2,1)}, bf16[1024,768]{1,0:T(8,128)(2,1)}, bf16[1024,768]{1,0:T(8,128)(2,1)}, bf16[1024,768]{1,0:T(8,128)(2,1)}, bf16[1024,768]{1,0:T(8,128)(2,1)})) conditional(s32[]{:T(128)} %convert_element_type.211, (s32[1024,1]{1,0:T(8,128)S(1)}, bf16[144,768]{1,0:T(8,128)(2,1)S(1)}, bf16[144,768]{1,0:T(8,128)(2,1)S(1)}, ...), branch_computations={%region_1.2_spmd, %region_2.5_spmd} | conditional | flops 7055050240 | bytes 46245024 | solution.py:643
  120.3 13.7 %project.2 = (bf16[1024,768]{1,0:T(8,128)(2,1)}, bf16[1024,768]{1,0:T(8,128)(2,1)}, bf16[1024,768]{1,0:T(8,128)(2,1)}, bf16[1024,768]{1,0:T(8,128)(2,1)}, bf16[1024,768]{1,0:T(8,128)(2,1)}) custom-call(s32[1024,1]{1,0:T(8,128)S(1)} %get-tuple-element.251.slot_ref, bf16[144,768]{1,0:T(8,128)(2,1)S(1)} %get-tuple-element.252.rows_refs_0_, ...), custom_call_target="tpu_custom_call" | custom-call | flops 5435817984 | bytes 11010048 | tf_op jit(solution)/shard_map/cond/branch_0_fun/project/pallas_call | solution.py:126
  141.6 17.9 %attend.1 = (bf16[1024,768]{1,0:T(8,128)(2,1)}, bf16[2,12,512,512]{3,2,1,0:T(8,128)(2,1)}) custom-call(s32[2]{0:T(128)} %len_ref.1, f32[32,12]{1,0:T(8,128)} %copy.68.far_ref, bf16[1024,768]{1,0:T(8,128)(2,1)} %get-tuple-element.418.q_ref, bf16[1024,768]{1,0:T(8,128)(2,1)} %get-tuple-element.419.k_ref, bf16[1024,768]{1,0:T(8,128)(2,1)} %get-tuple-element.420.v_ref, ...), custom_call_target="tpu_custom_call" | custom-call | flops 6442450944 | bytes 12582912 | tf_op jit(solution)/shard_map/attend/pallas_call | solution.py:195
  159.6 34.4 %middle.1 = (bf16[1024,768]{1,0:T(8,128)(2,1)}, bf16[1024,3072]{1,0:T(8,128)(2,1)}, bf16[1024,3072]{1,0:T(8,128)(2,1)}, bf16[768,1024]{1,0:T(8,128)(2,1)}, f32[1...) custom-call(bf16[1024,768]{1,0:T(8,128)(2,1)S(1)} %copy-done.107, ...), custom_call_target="tpu_custom_call" | custom-call | flops 21743271936 | bytes 40894464 | tf_op jit(solution)/shard_map/middle/pallas_call | solution.py:341
  194.0 26.5 %attend_back.1 = (bf16[1024,768]{1,0:T(8,128)(2,1)}, bf16[1024,768]{1,0:T(8,128)(2,1)}, bf16[1024,768]{1,0:T(8,128)(2,1)}, f32[6,8,512]{2,1,0:T(8,128)}) custom-call(bf16[1024,768]{1,0:T(8,128)(2,1)S(1)} %copy-done.108, bf16[1024,768]{1,0:T(8,128)(2,1)S(1)} %copy-done.109, bf16[1024,768]{1,0:T(8,128)(2,1)} %get-tuple-element.420.v_ref, ...), custom_call_target="tpu_custom_call" | custom-call | flops 9663676416 | bytes 12582912 | tf_op jit(solution)/shard_map/attend_back/pallas_call | solution.py:274
  224.0 14.8 %rows_back.1 = (f32[1024,768]{1,0:T(8,128)}, f32[8,768]{1,0:T(8,128)}, bf16[144,768]{1,0:T(8,128)(2,1)}, bf16[144,768]{1,0:T(8,128)(2,1)}, bf16[144,768]{1,0:T(8...) custom-call(s32[1,1024]{1,0:T(1,128)} %get-tuple-element.423.slot_re, ...), custom_call_target="tpu_custom_call" | custom-call | flops 5435817984 | bytes 15728640 | tf_op jit(solution)/shard_map/rows_back/pallas_call | solution.py:468
  247.3 7.4 %square_grads.3 = (bf16[4,4,96,384]{3,2,1,0:T(8,128)(2,1)}, bf16[4,4,96,384]{3,2,1,0:T(8,128)(2,1)}) custom-call(s32[1]{0:T(128)} %bitcast.27.core_ref, bf16[1024,768]{1,0:T(8,128)(2,1)} %get-tuple-element.429.dv_ref.left_refs_0_, bf16[1024,768]{1,0:T(8,128)(2,1)} %get-tuple-element.445.left_refs_1_, ...), custom_call_target="tpu_custom_call" | custom-call | flops 2415919104 | bytes 9437184 | tf_op jit(solution)/shard_map/square_grads/pallas_call | solution.py:425
  254.7 11.2 %collective-permute-done.34 = f32[16,128]{1,0:T(8,128)S(1)} collective-permute-done((f32[16,128]{1,0:T(8,128)S(1)}, f32[16,128]{1,0:T(8,128)S(1)}, u32[]{:S(2)}, u32[]{:S(2)}) %collective-permute-start.34) | collective-permute-done | bytes 8224 | tf_op jit(solution)/shard_map/ppermute | solution.py:513
  270.3 11.3 %collective-permute-done.20 = bf16[144,768]{1,0:T(8,128)(2,1)S(1)} collective-permute-done((bf16[144,768]{1,0:T(8,128)(2,1)S(1)}, bf16[144,768]{1,0:T(8,128)(2,1)S(1)}, u32[]{:S(2)}, u32[]{:S(2)}) %collective-permute-start.20) | collective-permute-done | bytes 221216 | tf_op jit(solution)/shard_map/ppermute | solution.py:513
  291.2 6.0 %collective-permute-done.15 = bf16[144,768]{1,0:T(8,128)(2,1)S(1)} collective-permute-done((bf16[144,768]{1,0:T(8,128)(2,1)S(1)}, bf16[144,768]{1,0:T(8,128)(2,1)S(1)}, u32[]{:S(2)}, u32[]{:S(2)}) %collective-permute-start.15) | collective-permute-done | bytes 221216 | tf_op jit(solution)/shard_map/ppermute | solution.py:513
  316.1 7.4 %square_grads.2 = (bf16[4,4,96,384]{3,2,1,0:T(8,128)(2,1)}, bf16[4,4,96,384]{3,2,1,0:T(8,128)(2,1)}) custom-call(s32[1]{0:T(128)} %bitcast.27.core_ref, bf16[1024,768]{1,0:T(8,128)(2,1)} %get-tuple-element.427.dq_ref.left_refs_0_, bf16[1024,768]{1,0:T(8,128)(2,1)} %get-tuple-element.428.dk_ref.left_refs_1_, ...), custom_call_target="tpu_custom_call" | custom-call | flops 2415919104 | bytes 9437184 | tf_op jit(solution)/shard_map/square_grads/pallas_call | solution.py:425
  329.4 21.0 %wide_grads.1 = (bf16[4,4,192,384]{3,2,1,0:T(8,128)(2,1)}, bf16[4,4,192,384]{3,2,1,0:T(8,128)(2,1)}, bf16[4,4,2,96,384]{4,3,2,1,0:T(8,128)(2,1)}, bf16[4,4,2,96,384]{4,3,2,1,0:T(8,128)(2,1)}) custom-call(s32[1]{0:T(128)} %bitcast.27.core_ref, bf16[768,1024]{1,0:T(8,128)(2,1)} %get-tuple-element.448.hidden_t_ref, bf16[768,1024]{1,0:T(8,128)(2,1)} %bitcast.162, ...), custom_call_target="tpu_custom_call" | custom-call | flops 9663676416 | bytes 22020096 | tf_op jit(solution)/shard_map/wide_grads/pallas_call | solution.py:392
  380.2 12.0 %collective-permute-done.12 = bf16[144,768]{1,0:T(8,128)(2,1)S(1)} collective-permute-done((bf16[144,768]{1,0:T(8,128)(2,1)S(1)}, bf16[144,768]{1,0:T(8,128)(2,1)S(1)}, u32[]{:S(2)}, u32[]{:S(2)}) %collective-permute-start.12) | collective-permute-done | bytes 221216 | tf_op jit(solution)/shard_map/ppermute | solution.py:513
  392.3 62.1 %conditional.3 = (f32[4016,768]{1,0:T(8,128)}) conditional(s32[]{:T(128)} %convert_element_type.211, (s32[1,288]{1,0:T(1,128)S(1)}, s32[1,288]{1,0:T(1,128)S(1)}, s32[1,288]{1,0:T(1,128)S(1)}, s32[1,144]{1,0:T(1,128)S(1)}, s32[1,144]{1,0:T(1,128)S(1)}, /*index=5*/s32[1,288]{1,0:T(1,128)S(1)}, s32[1,288]{1,0:T(1,128)S(1)}, s32[1,288]{1,0:T(1,128)S(1)}, ...), branch_computations={%region_5.6_spmd, %region_6.12_spmd} | conditional | flops 28439465984 | bytes 164639744 | solution.py:691
  392.3 57.4 %place_rows.2 = f32[4016,768]{1,0:T(8,128)} custom-call(s32[1,288]{1,0:T(1,128)S(1)} %get-tuple-element.280.target_refs_0_, s32[1,288]{1,0:T(1,128)S(1)} %get-tuple-element.281.target_refs_1_, s32[1,288]{1,0:T(1,128)S(1)} %get-tuple-element.282.target_refs_2_, s32[1,144]{1,0:T(1,128)S(1)} %get-tuple-element.283.target_refs_3_, ...), custom_call_target="tpu_custom_call" | custom-call | flops 28424798208 | bytes 19415040 | tf_op jit(solution)/shard_map/cond/branch_0_fun/place_rows/pallas_call | solution.py:499
  488.3 7.3 %collective-permute-done.56 = bf16[2,4,2,96,384]{4,3,2,1,0:T(8,128)(2,1)} collective-permute-done((bf16[2,4,2,96,384]{4,3,2,1,0:T(8,128)(2,1)S(1)}, bf16[2,4,2,96,384]{4,3,2,1,0:T(8,128)(2,1)}, u32[]{:S(2)}, u32[]{:S(2)}) %collective-permute-start.56) | collective-permute-done | bytes 1179680 | tf_op jit(solution)/shard_map/ppermute | solution.py:513
  499.4 5.3 collective-permute-done.50
  527.1 10.6 %collective-permute-done.59 = bf16[2,96,384]{2,1,0:T(8,128)(2,1)S(1)} collective-permute-done((bf16[2,96,384]{2,1,0:T(8,128)(2,1)S(1)}, bf16[2,96,384]{2,1,0:T(8,128)(2,1)S(1)}, u32[]{:S(2)}, u32[]{:S(2)}) %collective-permute-start.59) | collective-permute-done | bytes 147488 | tf_op jit(solution)/shard_map/ppermute | solution.py:513
  (335 shorter events, 210.1 us)
Async XLA Ops:
  38.4 42.7 %collective-permute-start.1 = (s32[2,8,256]{2,1,0:T(8,128)S(1)}, s32[2,8,256]{2,1,0:T(8,128)S(1)}, u32[]{:S(2)}, u32[]{:S(2)}) collective-permute-start(s32[2,8,256]{2,1,0:T(8,128)S(1)} %pad_add_fusion.1), channel_id=1, source_target_pairs={{0,16},{8,24},{16,0},{24,8},{1,17},{9,25},{17,1},{25,9},{2,18},{10... | collective-permute-start | bytes 49160 | tf_op jit(solution)/shard_map/ppermute | solution.py:513
  80.5 28.2 %collective-permute-start.5 = (bf16[144,768]{1,0:T(8,128)(2,1)S(1)}, bf16[144,768]{1,0:T(8,128)(2,1)S(1)}, u32[]{:S(2)}, u32[]{:S(2)}) collective-permute-start(bf16[144,768]{1,0:T(8,128)(2,1)S(1)} %gather_fusion.7), channel_id=1, source_target_pairs={{0,4},{1,5},{2,6},{3,7},{4,0},{5,1},{6,2},{7,3},{8,12},{9,13},{10,... | collective-permute-start | bytes 663560 | tf_op jit(solution)/shard_map/ppermute | solution.py:513
  80.5 28.3 %collective-permute-start.3 = (bf16[144,768]{1,0:T(8,128)(2,1)S(1)}, bf16[144,768]{1,0:T(8,128)(2,1)S(1)}, u32[]{:S(2)}, u32[]{:S(2)}) collective-permute-start(bf16[144,768]{1,0:T(8,128)(2,1)S(1)} %gather_fusion.5), channel_id=1, source_target_pairs={{0,2},{1,3},{2,0},{3,1},{4,6},{5,7},{6,4},{7,5},{8,10},{9,11},{10,... | collective-permute-start | bytes 663560 | tf_op jit(solution)/shard_map/ppermute | solution.py:513
  81.1 27.6 %collective-permute-start.2 = (bf16[144,768]{1,0:T(8,128)(2,1)S(1)}, bf16[144,768]{1,0:T(8,128)(2,1)S(1)}, u32[]{:S(2)}, u32[]{:S(2)}) collective-permute-start(bf16[144,768]{1,0:T(8,128)(2,1)S(1)} %gather_fusion.4), channel_id=1, source_target_pairs={{0,1},{1,0},{2,3},{3,2},{4,5},{5,4},{6,7},{7,6},{8,9},{9,8},{10,11... | collective-permute-start | bytes 663560 | tf_op jit(solution)/shard_map/ppermute | solution.py:513
  81.2 27.6 %collective-permute-start.8 = (bf16[144,768]{1,0:T(8,128)(2,1)S(1)}, bf16[144,768]{1,0:T(8,128)(2,1)S(1)}, u32[]{:S(2)}, u32[]{:S(2)}) collective-permute-start(bf16[144,768]{1,0:T(8,128)(2,1)S(1)} %gather_fusion.10), channel_id=1, source_target_pairs={{0,7},{1,6},{2,5},{3,4},{4,3},{5,2},{6,1},{7,0},{8,15},{9,14},{10,... | collective-permute-start | bytes 663560 | tf_op jit(solution)/shard_map/ppermute | solution.py:513
  86.9 29.7 %collective-permute-start.6 = (bf16[144,768]{1,0:T(8,128)(2,1)S(1)}, bf16[144,768]{1,0:T(8,128)(2,1)S(1)}, u32[]{:S(2)}, u32[]{:S(2)}) collective-permute-start(bf16[144,768]{1,0:T(8,128)(2,1)S(1)} %gather_fusion.8), channel_id=1, source_target_pairs={{0,5},{1,4},{2,7},{3,6},{4,1},{5,0},{6,3},{7,2},{8,13},{9,12},{10,... | collective-permute-start | bytes 663560 | tf_op jit(solution)/shard_map/ppermute | solution.py:513
  241.8 48.7 %collective-permute-start.9 = (bf16[144,768]{1,0:T(8,128)(2,1)}, bf16[144,768]{1,0:T(8,128)(2,1)S(1)}, u32[]{:S(2)}, u32[]{:S(2)}) collective-permute-start(bf16[144,768]{1,0:T(8,128)(2,1)} %get-tuple-element.432), channel_id=1, source_target_pairs={{0,1},{1,0},{2,3},{3,2},{4,5},{5,4},{6,7},{7,6},{8,9},{9,8},{10,11... | collective-permute-start | bytes 663560 | tf_op jit(solution)/shard_map/ppermute | solution.py:513
  241.9 47.7 %collective-permute-start.14 = (bf16[144,768]{1,0:T(8,128)(2,1)}, bf16[144,768]{1,0:T(8,128)(2,1)S(1)}, u32[]{:S(2)}, u32[]{:S(2)}) collective-permute-start(bf16[144,768]{1,0:T(8,128)(2,1)} %get-tuple-element.433), channel_id=1, source_target_pairs={{0,2},{1,3},{2,0},{3,1},{4,6},{5,7},{6,4},{7,5},{8,10},{9,11},{10,... | collective-permute-start | bytes 663560 | tf_op jit(solution)/shard_map/ppermute | solution.py:513
  244.8 23.3 %collective-permute-start.27 = (bf16[144,768]{1,0:T(8,128)(2,1)}, bf16[144,768]{1,0:T(8,128)(2,1)S(1)}, u32[]{:S(2)}, u32[]{:S(2)}) collective-permute-start(bf16[144,768]{1,0:T(8,128)(2,1)} %get-tuple-element.438), channel_id=1, source_target_pairs={{0,7},{1,6},{2,5},{3,4},{4,3},{5,2},{6,1},{7,0},{8,15},{9,14},{10,... | collective-permute-start | bytes 663560 | tf_op jit(solution)/shard_map/ppermute | solution.py:513
  281.7 23.4 %collective-permute-start.29 = (bf16[288,768]{1,0:T(8,128)(2,1)}, bf16[288,768]{1,0:T(8,128)(2,1)}, u32[]{:S(2)}, u32[]{:S(2)}) collective-permute-start(bf16[288,768]{1,0:T(8,128)(2,1)} %constant_dynamic-update-slice_fusion.6), channel_id=1, source_target_pairs={{0,16},{8,24},{16,0},{24,8},{1,17},{9,25},{17,1},{25,9},{2,18},{10... | collective-permute-start | bytes 1327112 | tf_op jit(solution)/shard_map/ppermute | solution.py:513
  290.5 71.0 %collective-permute-start.43 = (bf16[4,4,96,384]{3,2,1,0:T(8,128)(2,1)}, bf16[4,4,96,384]{3,2,1,0:T(8,128)(2,1)S(1)}, u32[]{:S(2)}, u32[]{:S(2)}) collective-permute-start(bf16[4,4,96,384]{3,2,1,0:T(8,128)(2,1)} %get-tuple-element.447), channel_id=1, source_target_pairs={{0,1},{1,0},{2,3},{3,2},{4,5},{5,4},{6,7},{7,6},{8,9},{9,8},{10,11... | collective-permute-start | bytes 3538952 | tf_op jit(solution)/shard_map/ppermute | solution.py:513
  303.6 23.2 %collective-permute-start.22 = (bf16[288,768]{1,0:T(8,128)(2,1)}, bf16[288,768]{1,0:T(8,128)(2,1)}, u32[]{:S(2)}, u32[]{:S(2)}) collective-permute-start(bf16[288,768]{1,0:T(8,128)(2,1)} %constant_dynamic-update-slice_fusion.4), channel_id=1, source_target_pairs={{0,8},{8,0},{16,24},{24,16},{1,9},{9,1},{17,25},{25,17},{2,10},{10... | collective-permute-start | bytes 1327112 | tf_op jit(solution)/shard_map/ppermute | solution.py:513
  305.6 22.8 %collective-permute-start.16 = (bf16[288,768]{1,0:T(8,128)(2,1)}, bf16[288,768]{1,0:T(8,128)(2,1)}, u32[]{:S(2)}, u32[]{:S(2)}) collective-permute-start(bf16[288,768]{1,0:T(8,128)(2,1)} %constant_dynamic-update-slice_fusion.2), channel_id=1, source_target_pairs={{0,8},{8,0},{16,24},{24,16},{1,9},{9,1},{17,25},{25,17},{2,10},{10... | collective-permute-start | bytes 1327112 | tf_op jit(solution)/shard_map/ppermute | solution.py:513
  306.1 22.8 %collective-permute-start.11 = (bf16[288,768]{1,0:T(8,128)(2,1)}, bf16[288,768]{1,0:T(8,128)(2,1)}, u32[]{:S(2)}, u32[]{:S(2)}) collective-permute-start(bf16[288,768]{1,0:T(8,128)(2,1)} %constant_dynamic-update-slice_fusion), channel_id=1, source_target_pairs={{0,16},{8,24},{16,0},{24,8},{1,17},{9,25},{17,1},{25,9},{2,18},{10... | collective-permute-start | bytes 1327112 | tf_op jit(solution)/shard_map/ppermute | solution.py:513
  326.8 45.8 %collective-permute-start.37 = (bf16[4,4,96,384]{3,2,1,0:T(8,128)(2,1)}, bf16[4,4,96,384]{3,2,1,0:T(8,128)(2,1)S(1)}, u32[]{:S(2)}, u32[]{:S(2)}) collective-permute-start(bf16[4,4,96,384]{3,2,1,0:T(8,128)(2,1)} %get-tuple-element.444), channel_id=1, source_target_pairs={{0,1},{1,0},{2,3},{3,2},{4,5},{5,4},{6,7},{7,6},{8,9},{9,8},{10,11... | collective-permute-start | bytes 3538952 | tf_op jit(solution)/shard_map/ppermute | solution.py:513
  326.8 30.6 %collective-permute-start.10 = (bf16[288,768]{1,0:T(8,128)(2,1)}, bf16[288,768]{1,0:T(8,128)(2,1)}, u32[]{:S(2)}, u32[]{:S(2)}) collective-permute-start(bf16[288,768]{1,0:T(8,128)(2,1)} %constant_dynamic-update-slice_fusion), channel_id=1, source_target_pairs={{0,8},{8,0},{16,24},{24,16},{1,9},{9,1},{17,25},{25,17},{2,10},{10... | collective-permute-start | bytes 1327112 | tf_op jit(solution)/shard_map/ppermute | solution.py:513
  328.3 30.0 %collective-permute-start.31 = (bf16[144,768]{1,0:T(8,128)(2,1)}, bf16[144,768]{1,0:T(8,128)(2,1)}, u32[]{:S(2)}, u32[]{:S(2)}) collective-permute-start(bf16[144,768]{1,0:T(8,128)(2,1)} %slice.380), channel_id=1, source_target_pairs={{0,8},{8,0},{16,24},{24,16},{1,9},{9,1},{17,25},{25,17},{2,10},{10... | collective-permute-start | bytes 663560 | tf_op jit(solution)/shard_map/ppermute | solution.py:513
  328.9 31.1 %collective-permute-start.30 = (bf16[144,768]{1,0:T(8,128)(2,1)}, bf16[144,768]{1,0:T(8,128)(2,1)}, u32[]{:S(2)}, u32[]{:S(2)}) collective-permute-start(bf16[144,768]{1,0:T(8,128)(2,1)} %slice.379), channel_id=1, source_target_pairs={{0,16},{8,24},{16,0},{24,8},{1,17},{9,25},{17,1},{25,9},{2,18},{10... | collective-permute-start | bytes 663560 | tf_op jit(solution)/shard_map/ppermute | solution.py:513
  357.3 110.3 %collective-permute-start.55 = (bf16[4,4,2,96,384]{4,3,2,1,0:T(8,128)(2,1)}, bf16[4,4,2,96,384]{4,3,2,1,0:T(8,128)(2,1)}, u32[]{:S(2)}, u32[]{:S(2)}) collective-permute-start(bf16[4,4,2,96,384]{4,3,2,1,0:T(8,128)(2,1)} %get-tuple-element.454), channel_id=1, source_target_pairs={{0,1},{1,0},{2,3},{3,2},{4,5},{5,4},{6,7},{7,6},{8,9},{9,8},{10,11... | collective-permute-start | bytes 7077896 | tf_op jit(solution)/shard_map/ppermute | solution.py:513
  366.7 105.2 %collective-permute-start.49 = (bf16[4,4,192,384]{3,2,1,0:T(8,128)(2,1)}, bf16[4,4,192,384]{3,2,1,0:T(8,128)(2,1)}, u32[]{:S(2)}, u32[]{:S(2)}) collective-permute-start(bf16[4,4,192,384]{3,2,1,0:T(8,128)(2,1)} %get-tuple-element.452), channel_id=1, source_target_pairs={{0,1},{1,0},{2,3},{3,2},{4,5},{5,4},{6,7},{7,6},{8,9},{9,8},{10,11... | collective-permute-start | bytes 7077896 | tf_op jit(solution)/shard_map/ppermute | solution.py:513
  372.5 81.9 %collective-permute-start.44 = (bf16[2,4,96,384]{3,2,1,0:T(8,128)(2,1)}, bf16[2,4,96,384]{3,2,1,0:T(8,128)(2,1)}, u32[]{:S(2)}, u32[]{:S(2)}) collective-permute-start(bf16[2,4,96,384]{3,2,1,0:T(8,128)(2,1)} %dynamic-slice_bitcast_fusion.4), channel_id=1, source_target_pairs={{0,16},{8,24},{16,0},{24,8},{1,17},{9,25},{17,1},{25,9},{2,18},{10... | collective-permute-start | bytes 1769480 | tf_op jit(solution)/shard_map/ppermute | solution.py:513
  378.1 79.3 %collective-permute-start.38 = (bf16[2,4,96,384]{3,2,1,0:T(8,128)(2,1)S(1)}, bf16[2,4,96,384]{3,2,1,0:T(8,128)(2,1)}, u32[]{:S(2)}, u32[]{:S(2)}) collective-permute-start(bf16[2,4,96,384]{3,2,1,0:T(8,128)(2,1)S(1)} %dynamic-slice_bitcast_fusion.5), channel_id=1, source_target_pairs={{0,8},{8,0},{16,24},{24,16},{1,9},{9,1},{17,25},{25,17},{2,10},{10... | collective-permute-start | bytes 1769480 | tf_op jit(solution)/shard_map/ppermute | solution.py:513
  470.3 25.3 %collective-permute-start.56 = (bf16[2,4,2,96,384]{4,3,2,1,0:T(8,128)(2,1)S(1)}, bf16[2,4,2,96,384]{4,3,2,1,0:T(8,128)(2,1)}, u32[]{:S(2)}, u32[]{:S(2)}) collective-permute-start(bf16[2,4,2,96,384]{4,3,2,1,0:T(8,128)(2,1)S(1)} %dynamic-slice_bitcast_fusion), channel_id=1, source_target_pairs={{0,16},{8,24},{16,0},{24,8},{1,17},{9,25},{17,1},{25,9},{2,18},{10... | collective-permute-start | bytes 3538952 | tf_op jit(solution)/shard_map/ppermute | solution.py:513
  475.5 29.2 %collective-permute-start.50 = (bf16[2,4,192,384]{3,2,1,0:T(8,128)(2,1)}, bf16[2,4,192,384]{3,2,1,0:T(8,128)(2,1)}, u32[]{:S(2)}, u32[]{:S(2)}) collective-permute-start(bf16[2,4,192,384]{3,2,1,0:T(8,128)(2,1)} %dynamic-slice_bitcast_fusion.1), channel_id=1, source_target_pairs={{0,8},{8,0},{16,24},{24,16},{1,9},{9,1},{17,25},{25,17},{2,10},{10... | collective-permute-start | bytes 3538952 | tf_op jit(solution)/shard_map/ppermute | solution.py:513
  (85 other events, 1400.6 us)
